TPU v7x, 128 devices: a whole 4x4x4 slice. The times are simulated.
128 devices in a mesh: rows: 64 (over x, z, y), cols: 2 (over core).
Axes of the slice: x: 4, y: 4, z: 4, core: 2. Of those that a mesh axis runs over, the one named last changes fastest.
Arguments:
- blocks: bfloat16 [4096, 7, 128, 128], P('rows'), may hold values from -0.1875 to 0.1875
- col_index: int32 [4096, 7], P('rows'), may hold values from 0 to 4095, as said below
- right_vecs: bfloat16 [64, 4096, 128], P('cols', 'rows'), may hold values from -30 to 30
- left_vecs: bfloat16 [64, 4096, 128], P('cols', 'rows'), may hold values from -30 to 30
- ritz: bfloat16 [64, 64], replicated, may hold values from -0.75 to 0.75
Outputs:
- right_res: float32 [64, 4096, 128], P('cols', 'rows')
- left_res: float32 [64, 4096, 128], P('cols', 'rows')
- right_norms: float32 [64], P('cols')
- left_norms: float32 [64], P('cols')
Inputs may be any that keep to these rules, and one draw needn't show every extreme that they name: `col_index`: entry 0 of each block row is the row's own index. Device p of rows holds block rows p * 64 to (p + 1) * 64 - 1. The devices form a grid of 2 x (32) subdomains of the slab, p = i * M + j with M = 32, periodic along j. Columns outside a device's own rows lie only on its three face neighbours: (i, j + 1 mod M), (i, j - 1 mod M) and (1 - i, j). Among the entries of one device's block rows exactly 2 have a column on (i, j + 1 mod M), and 1 to 2 on each of the other two.
All inputs are finite; a program needn't handle non-finite values.
Results may differ from a plain program's by a relative error of at most 0.0006.
Values may be sent and summed in bfloat16 or wider, within the bound.
A program may use at most 128 MiB of HBM per device.

v0:
```python
import jax
import jax.numpy as jnp
from jax import lax
from jax.sharding import PartitionSpec as P

SENDS = 2


def shards(blocks, col_index, right_vecs, left_vecs, ritz):
    peers = lax.axis_size("rows")
    me = lax.axis_index("rows")
    rows_here = col_index.shape[0]
    slots = col_index.shape[1]
    vec_here = right_vecs.shape[0]
    width = right_vecs.shape[2]
    owner = (col_index // rows_here).reshape(-1)
    local_id = (col_index % rows_here).reshape(-1)
    remote = owner != me
    onehot = (owner[:, None] == jnp.arange(peers, dtype=jnp.int32)[None, :]).astype(jnp.int32)
    rank = jnp.sum(jnp.cumsum(onehot, axis=0) * onehot, axis=1) - 1
    ext_index = jnp.where(remote, rows_here + owner * SENDS + rank, local_id)
    target = jnp.where(remote, owner, peers)
    wanted = jnp.zeros((peers, SENDS), jnp.int32).at[target, rank].set(local_id, mode="drop")
    asked = lax.all_to_all(wanted, "rows", split_axis=0, concat_axis=0, tiled=True)
    asked_flat = asked.reshape(-1)
    outgoing = right_vecs[:, asked_flat, :]
    contrib = jnp.einsum("kra,rsab->krsb", left_vecs, blocks, preferred_element_type=jnp.float32)
    contrib = contrib.reshape(vec_here, rows_here * slots, width)
    summed = (
        jnp.zeros((vec_here, rows_here + peers * SENDS, width), jnp.float32)
        .at[:, ext_index, :]
        .add(contrib)
    )
    incoming = lax.all_to_all(outgoing, "rows", split_axis=1, concat_axis=1, tiled=True)
    returned = lax.all_to_all(
        summed[:, rows_here:, :].astype(jnp.bfloat16),
        "rows",
        split_axis=1,
        concat_axis=1,
        tiled=True,
    ).astype(jnp.float32)
    extended = jnp.concatenate([right_vecs, incoming], axis=1)
    gathered = extended[:, ext_index, :].reshape(vec_here, rows_here, slots, width)
    product = jnp.einsum("krsj,rsij->kri", gathered, blocks, preferred_element_type=jnp.float32)
    transposed = summed[:, :rows_here, :].at[:, asked_flat, :].add(returned)
    mine = lax.axis_index("cols") * vec_here
    full_right, full_left = (
        lax.all_gather(right_vecs, "cols", axis=0, tiled=True),
        lax.all_gather(left_vecs, "cols", axis=0, tiled=True),
    )
    total = ritz.shape[0]
    right_table = lax.dynamic_slice(ritz, (0, mine), (total, vec_here))
    left_table = lax.dynamic_slice(ritz.T, (0, mine), (total, vec_here))
    right_shift = jnp.einsum(
        "krb,kq->qrb", full_right, right_table, preferred_element_type=jnp.float32
    )
    left_shift = jnp.einsum(
        "krb,kq->qrb", full_left, left_table, preferred_element_type=jnp.float32
    )
    right_res = product - right_shift
    left_res = transposed - left_shift
    right_sq, left_sq = lax.psum(
        (jnp.sum(right_res * right_res, axis=(1, 2)), jnp.sum(left_res * left_res, axis=(1, 2))),
        "rows",
    )
    return (right_res, left_res, jnp.sqrt(right_sq), jnp.sqrt(left_sq))


def solution(mesh):
    placed = (
        P("rows", None, None, None),
        P("rows", None),
        P("cols", "rows", None),
        P("cols", "rows", None),
        P(),
    )
    return jax.shard_map(
        shards,
        mesh=mesh,
        in_specs=placed,
        out_specs=(P("cols", "rows", None), P("cols", "rows", None), P("cols"), P("cols")),
        check_vma=False,
    )
```

profile of v0, /device:TPU:0, one launch (start us, length us, event | category | flops | bytes accessed | tf_op | source)
XLA Modules:
  0.0 374.1 jit_solution(11511773437690598463)
XLA Ops:
  7.2 0.8 add_select_fusion
  8.8 1.2 reduce-window.6
  10.4 21.3 %scatter_fusion = s32[64,2]{0,1:T(2,128)S(1)} fusion(s32[64,2]{0,1:T(2,128)S(1)} %broadcast_in_dim.8, s32[448]{0:T(512)S(1)} %bitcast.54, s32[448]{0:T(512)S(1)} %reshape.185), kind=kCustom, calls=%fused_computation.2 | custom fusion | bytes 8960 | tf_op jit(solution)/shard_map/scatter | solution.py:23
  31.7 0.7 copy.36
  32.5 11.5 %all-to-all-start = ((s32[64,1,2]{2,1,0:T(1,128)}), s32[64,1,2]{2,1,0:T(1,128)S(1)}, u32[]{:S(2)}, u32[]{:S(2)}) async-start(s32[64,1,2]{2,1,0:T(1,128)} %copy.36), calls=%async_computation | async-start | bytes 65536 | tf_op jit(solution)/shard_map/all_to_all | solution.py:24
  44.0 10.5 %fusion = f32[64,7,128,32]{2,3,1,0:T(8,128)} fusion(bf16[64,7,128,128]{3,2,1,0:T(8,128)(2,1)} %param.5, bf16[32,64,128,1]{2,1,0,3:T(8,128)(2,1)S(1)} %bitcast.57), kind=kOutput, calls=%fused_computation.13 | convolution fusion | flops 469762048 | bytes 22544384 | tf_op jit(solution)/shard_map/kra,rsab->krsb/dot_general | solution.py:27
  54.5 2.1 broadcast_in_dim.10
  56.6 59.7 %scatter_fusion.1 = f32[32,192,128]{2,0,1:T(8,128)} fusion(f32[32,192,128]{2,0,1:T(8,128)} %broadcast_in_dim.10, s32[448]{0:T(512)S(1)} %bitcast.58, f32[448,32,128]{2,1,0:T(8,128)} %bitcast.53), kind=kCustom, calls=%fused_computation.3 | custom fusion | flops 1835008 | bytes 22021888 | tf_op jit(solution)/shard_map/scatter-add | solution.py:32
  116.3 2.8 slice.36
  119.1 10.3 %all-to-all-start.2 = ((bf16[32,128,128]{2,0,1:T(8,128)(2,1)}), bf16[32,128,128]{2,0,1:T(8,128)(2,1)S(1)}, u32[]{:S(2)}, u32[]{:S(2)}) async-start(bf16[32,128,128]{2,0,1:T(8,128)(2,1)} %slice.36), calls=%async_computation.2 | async-start | bytes 2097152 | tf_op jit(solution)/shard_map/all_to_all | solution.py:35
  129.6 1.1 copy.43
  130.8 0.5 broadcast.201
  131.3 0.7 reduce.5
  132.2 5.2 %gather_fusion = bf16[128,32,128]{2,0,1:T(8,128)(2,1)S(1)} fusion(bf16[32,64,128]{2,1,0:T(8,128)(2,1)S(1)} %copy-done.1, s32[1024]{0:T(1024)S(1)} %pad_clamp_fusion.1), kind=kCustom, calls=%fused_computation | custom fusion | bytes 2097664 | tf_op jit(solution)/shard_map/gather | solution.py:26
  137.4 1.6 copy.37
  139.1 8.3 %all-to-all-done.2 = bf16[32,128,128]{2,0,1:T(8,128)(2,1)S(1)} async-done(((bf16[32,128,128]{2,0,1:T(8,128)(2,1)}), bf16[32,128,128]{2,0,1:T(8,128)(2,1)S(1)}, u32[]{:S(2)}, u32[]{:S(2)}) %all-to-all-start.2) | async-done | bytes 1048608 | tf_op jit(solution)/shard_map/all_to_all | solution.py:35
  147.4 5.5 %all-to-all-start.1 = ((bf16[32,128,128]{2,0,1:T(8,128)(2,1)}), bf16[32,128,128]{2,0,1:T(8,128)(2,1)}, u32[]{:S(2)}, u32[]{:S(2)}) async-start(bf16[32,128,128]{2,0,1:T(8,128)(2,1)} %copy.37), calls=%async_computation.1 | async-start | bytes 2097152 | tf_op jit(solution)/shard_map/all_to_all | solution.py:34
  153.0 1.2 copy.38
  154.1 1.3 slice.29
  155.5 1.5 convert_bitcast_fusion
  157.0 5.9 %scatter_fusion.2 = f32[32,64,128]{2,0,1:T(8,128)S(1)} fusion(f32[32,64,128]{2,0,1:T(8,128)S(1)} %slice.29, s32[128]{0:T(128)S(1)} %fusion.10, f32[128,32,128]{2,1,0:T(8,128)S(1)} %convert_bitcast_fusion), kind=kCustom, calls=%fused_computation.4 | custom fusion | flops 524288 | bytes 6291968 | tf_op jit(solution)/shard_map/scatter-add | solution.py:45
  162.9 6.7 %all-to-all-done.1 = bf16[32,128,128]{2,0,1:T(8,128)(2,1)} async-done(((bf16[32,128,128]{2,0,1:T(8,128)(2,1)}), bf16[32,128,128]{2,0,1:T(8,128)(2,1)}, u32[]{:S(2)}, u32[]{:S(2)}) %all-to-all-start.1) | async-done | bytes 1048608 | tf_op jit(solution)/shard_map/all_to_all | solution.py:34
  169.6 1.5 pad_maximum_fusion
  171.1 3.4 gather_fusion.1
  174.5 11.4 %convolution_bitcast_fusion = f32[32,64,128]{2,0,1:T(8,128)S(1)} fusion(bf16[32,64,7,128]{3,0,2,1:T(8,128)(2,1)} %bitcast.55, bf16[64,7,128,128]{3,2,1,0:T(8,128)(2,1)} %param.5), kind=kOutput, calls=%fused_computation.10 | convolution fusion | flops 469762048 | bytes 19398656 | tf_op jit(solution)/shard_map/krsj,rsij->kri/dot_general | solution.py:44
  185.9 1.6 multiply_reduce_fusion
  187.6 1.7 multiply_reduce_fusion.1
  189.3 173.7 %all-reduce.1 = (f32[32]{0:T(128)S(1)}, f32[32]{0:T(128)S(1)}) all-reduce(f32[32]{0:T(128)S(1)} %get-tuple-element.24, f32[32]{0:T(128)S(1)} %get-tuple-element.26), channel_id=1, replica_groups=mesh['rows'=64,'cols'=2] {'rows'}, use_global_device_ids=true, to_apply=%region_7.8 | all-reduce | flops 64 | bytes 512 | tf_op jit(solution)/shard_map/psum | solution.py:62
  363.1 0.5 sqrt.6
  363.6 0.5 sqrt.7
  364.1 1.6 copy.45
  365.7 1.6 copy.44
  (35 shorter events, 1.7 us)
Async XLA Ops:
  7.2 178.8 %copy-start = (bf16[64,64]{1,0:T(8,128)(2,1)S(1)}, bf16[64,64]{1,0:T(8,128)(2,1)}, u32[]{:S(2)}) copy-start(bf16[64,64]{1,0:T(8,128)(2,1)} %param.9) | copy-start | bytes 24580
  7.2 36.8 %copy-start.3 = (bf16[32,64,128]{2,1,0:T(8,128)(2,1)S(1)}, bf16[32,64,128]{2,1,0:T(8,128)(2,1)}, u32[]{:S(2)}) copy-start(bf16[32,64,128]{2,1,0:T(8,128)(2,1)} %param.8) | copy-start | bytes 1572868
  32.5 86.6 %all-to-all-start = ((s32[64,1,2]{2,1,0:T(1,128)}), s32[64,1,2]{2,1,0:T(1,128)S(1)}, u32[]{:S(2)}, u32[]{:S(2)}) async-start(s32[64,1,2]{2,1,0:T(1,128)} %copy.36), calls=%async_computation | async-start | bytes 65536 | tf_op jit(solution)/shard_map/all_to_all | solution.py:24
  116.3 15.9 %copy-start.1 = (bf16[32,64,128]{2,1,0:T(8,128)(2,1)S(1)}, bf16[32,64,128]{2,1,0:T(8,128)(2,1)}, u32[]{:S(2)}) copy-start(bf16[32,64,128]{2,1,0:T(8,128)(2,1)} %param.7) | copy-start | bytes 1572868
  119.1 28.3 %all-to-all-start.2 = ((bf16[32,128,128]{2,0,1:T(8,128)(2,1)}), bf16[32,128,128]{2,0,1:T(8,128)(2,1)S(1)}, u32[]{:S(2)}, u32[]{:S(2)}) async-start(bf16[32,128,128]{2,0,1:T(8,128)(2,1)} %slice.36), calls=%async_computation.2 | async-start | bytes 2097152 | tf_op jit(solution)/shard_map/all_to_all | solution.py:35
  129.4 56.5 %all-gather.5.cloned.1.call-start = ((), (), s32[]{:S(2)}) async-start(), calls=%async_computation.4 | async-start | bytes 1572864 | tf_op jit(solution)/shard_map/all_gather | solution.py:49
  147.4 6.7 %copy-start.2 = (bf16[32,128,128]{2,0,1:T(8,128)(2,1)}, bf16[32,128,128]{2,0,1:T(8,128)(2,1)S(1)}, u32[]{:S(2)}) copy-start(bf16[32,128,128]{2,0,1:T(8,128)(2,1)S(1)} %all-to-all-done.2) | copy-start | bytes 3145732
  147.4 22.2 %all-to-all-start.1 = ((bf16[32,128,128]{2,0,1:T(8,128)(2,1)}), bf16[32,128,128]{2,0,1:T(8,128)(2,1)}, u32[]{:S(2)}, u32[]{:S(2)}) async-start(bf16[32,128,128]{2,0,1:T(8,128)(2,1)} %copy.37), calls=%async_computation.1 | async-start | bytes 2097152 | tf_op jit(solution)/shard_map/all_to_all | solution.py:34
  152.9 34.7 %all-gather.3.cloned.1.call-start = ((), (), s32[]{:S(2)}) async-start(), calls=%async_computation.3 | async-start | bytes 1572864 | tf_op jit(solution)/shard_map/all_gather | solution.py:48
Sparse Core Ops, SparseCore 0:
  131.9 12.9 all-gather.4
  155.4 12.9 all-gather.2
where the time goes:
time: 375 us; the launch traced here: 374 us
  blocking collectives  174 us (46%)
  other arithmetic  71.6 us (19%)
  local copies, waits for them, and re-layouts  46.6 us (12%)
  starting transfers between devices  27.6 us (7%)
  matrix products  25.3 us (7%)
  waiting for transfers between devices  15.1 us (4%)
  between operations  14.3 us (4%)
    psum x1, blocking collectives, shards(): lax.psum((jnp.sum(right_res * right_res, axis=(1, 2)), jnp.sum(left_res *...  174 us
    scatter-add x1, other arithmetic, shards(): summed = jnp.zeros((vec_here, rows_here + peers * SENDS, width), jnp.floa...  59.7 us
    scatter x1, local copies, waits for them, and re-layouts, shards(): jnp.zeros((peers, SENDS), jnp.int32).at[target, rank]  21.3 us
    all_to_all x1, starting transfers between devices, shards(): lax.all_to_all(wanted, 'rows', split_axis=0, concat_axis=0, tiled=True)  11.5 us
    dot_general x1, matrix products, shards(): jnp.einsum('krsj,rsij->kri', gathered, blocks, preferred_element_type=jnp...  11.4 us
    dot_general x1, matrix products, shards(): jnp.einsum('kra,rsab->krsb', left_vecs, blocks, preferred_element_type=jn...  10.5 us
    all_to_all x1, starting transfers between devices, shards(): lax.all_to_all(summed[:, rows_here:, :].astype(jnp.bfloat16), 'rows', spl...  10.3 us
    all_to_all x1, waiting for transfers between devices, shards(): lax.all_to_all(summed[:, rows_here:, :].astype(jnp.bfloat16), 'rows', spl...  8.32 us
  transfers between devices with their start and end apart: 5, of which 2 were waited for; matrix products, arithmetic and copies ran while one was open for 30% of the time, Pallas kernels for 0%

commit v1 on v0

v1 whole, which is shorter than its diff:
```python
import functools

import jax
import jax.numpy as jnp
from jax import lax
from jax.experimental import pallas as pl
from jax.experimental.pallas import tpu as pltpu
from jax.sharding import PartitionSpec as P

MESH = pl.DeviceIdType.MESH
F32 = jnp.float32
BF16 = jnp.bfloat16
I32 = jnp.int32
SLOTS = 7
CHUNKS = 8
ROW_EXT, ROW_PREV, ROW_LAST, ROW_PICK, ROW_TWO = 0, 8, 16, 17, 24
BACK = (1, 0, 2)


def kernel(
    peers, rows, vecs,
    cols_hbm, blocks_hbm, x_hbm, y_hbm, ritz_hbm,
    right_hbm, left_hbm, norm_ref,
    cols, blk, raw, wide, xt, yt, xo, yo, summed, ritz, shift_r, shift_l,
    tab, tab_s, ask_out, ask_in, ask_s, x_out, x_in, t_out, t_in, back, lastc, lastc_s,
    right, left, acc, parts,
    in_sem, blk_sem, loc_sem, out_sem,
    ask_ss, ask_rs, x_ss, x_rs, t_ss, t_rs, o_ss, o_rs, n_ss, n_rs,
):
    me = lax.axis_index("rows")
    core = lax.axis_index("cols")
    half = peers // 2
    entries = rows * SLOTS
    layer, place = me // half, me % half
    near = (
        layer * half + (place + 1) % half,
        layer * half + (place + half - 1) % half,
        (me + half) % peers,
    )
    other = 1 - core
    side = (me // 16, (me // 4) % 4, me % 4)
    step = (16, 4, 1)

    def partner(stage, turn):
        return me + (lax.rem(side[stage] + turn, 4) - side[stage]) * step[stage]

    ins = [
        pltpu.make_async_copy(cols_hbm, cols, in_sem.at[0]),
        pltpu.make_async_copy(y_hbm, raw.at[0], in_sem.at[1]),
        pltpu.make_async_copy(x_hbm, raw.at[1], in_sem.at[2]),
        pltpu.make_async_copy(ritz_hbm, ritz, in_sem.at[3]),
    ]
    for copy in ins:
        copy.start()
    per_chunk = entries // CHUNKS

    def chunk_copy(c):
        span = pl.ds(c * per_chunk, per_chunk)
        return pltpu.make_async_copy(blocks_hbm.at[span], blk.at[span], blk_sem.at[c])

    def start_chunk(c, _):
        chunk_copy(c).start()
        return 0

    lax.fori_loop(0, CHUNKS, start_chunk, 0)

    barrier = pltpu.get_barrier_semaphore()
    for n in range(3):
        pl.semaphore_signal(barrier, inc=1, device_id=(near[n], core), device_id_type=MESH)
    pl.semaphore_signal(barrier, inc=1, device_id=(me, other), device_id_type=MESH)
    for stage in range(3):
        for turn in range(1, 4):
            pl.semaphore_signal(
                barrier, inc=1, device_id=(partner(stage, turn), core), device_id_type=MESH
            )

    ins[0].wait()
    col = cols[...]
    owner = col >> 6
    local = col & 63
    row_id = lax.broadcasted_iota(I32, (SLOTS, rows), 1)
    slot_id = lax.broadcasted_iota(I32, (SLOTS, rows), 0)
    order = row_id * SLOTS + slot_id

    def all_min(v):
        return jnp.min(jnp.min(v, axis=1, keepdims=True), axis=0, keepdims=True)

    def all_max(v):
        return jnp.max(jnp.max(v, axis=1, keepdims=True), axis=0, keepdims=True)

    ext = local
    for n in range(3):
        here = owner == near[n]
        first = all_min(jnp.where(here, order, entries))
        final = all_max(jnp.where(here, order, 0))
        id_first = all_max(jnp.where(order == first, local, 0))
        id_final = all_max(jnp.where(order == final, local, 0))
        ext = jnp.where(here, rows + 2 * n + (order == final).astype(I32), ext)
        ask_out[n, 0:1, :] = jnp.broadcast_to(id_first, (1, 128))
        ask_out[n, 1:2, :] = jnp.broadcast_to(id_final, (1, 128))
        ask_out[n, 2:8, :] = jnp.zeros((6, 128), I32)
        tab[ROW_PICK + 2 * n: ROW_PICK + 2 * n + 1, :] = jnp.broadcast_to(first, (1, 128))
        tab[ROW_PICK + 2 * n + 1: ROW_PICK + 2 * n + 2, :] = jnp.broadcast_to(final, (1, 128))
        tab[ROW_TWO + n: ROW_TWO + n + 1, :] = jnp.broadcast_to(
            (first != final).astype(I32), (1, 128)
        )
    tab[ROW_EXT: ROW_EXT + SLOTS, :rows] = ext

    pl.semaphore_wait(barrier, 13)
    asks = [
        pltpu.make_async_remote_copy(
            src_ref=ask_out.at[n], dst_ref=ask_in.at[BACK[n]],
            send_sem=ask_ss.at[n], recv_sem=ask_rs.at[BACK[n]],
            device_id=(near[n], core), device_id_type=MESH,
        )
        for n in range(3)
    ]
    for copy in asks:
        copy.start()

    col_t = jnp.transpose(
        jnp.concatenate([col.astype(F32), jnp.full((1, rows), -1.0, F32)], axis=0)
    ).astype(I32)
    src_row = lax.broadcasted_iota(I32, (rows, rows), 0)
    dst_row = lax.broadcasted_iota(I32, (rows, rows), 1)
    before, upto = src_row < dst_row, src_row <= dst_row
    src_order = src_row * SLOTS
    src_col = [jnp.broadcast_to(col_t[:, s:s + 1], (rows, rows)) for s in range(SLOTS)]
    for s in range(SLOTS):
        mine = jnp.broadcast_to(col[s:s + 1, :], (rows, rows))
        best = jnp.full((rows, rows), -1, I32)
        for t in range(SLOTS):
            best = jnp.where(
                (src_col[t] == mine) & (upto if t < s else before), src_order + t, best
            )
        found = jnp.max(best, axis=0, keepdims=True)
        found = jnp.where((found < 0) | (owner[s:s + 1, :] != me), entries, found)
        tab[ROW_PREV + s: ROW_PREV + s + 1, :rows] = found
    best = jnp.full((rows, rows), 0, I32)
    for t in range(SLOTS):
        best = jnp.where(src_col[t] == dst_row + me * rows, src_order + t, best)
    tab[ROW_LAST: ROW_LAST + 1, :rows] = jnp.max(best, axis=0, keepdims=True)
    tab_copy = pltpu.make_async_copy(tab, tab_s, loc_sem.at[0])
    tab_copy.start()

    def by_rows(index, dst):
        def widen(k, _):
            wide[pl.ds(k * rows, rows), :] = raw[index, k].astype(F32)
            return 0

        lax.fori_loop(0, vecs, widen, 0, unroll=4)

        def turn(r, _):
            dst[r] = wide[pl.ds(r, vecs, stride=rows), :].astype(BF16)
            return 0

        lax.fori_loop(0, rows, turn, 0, unroll=8)

    def across(src, dst, slot):
        return pltpu.make_async_remote_copy(
            src_ref=src, dst_ref=dst, send_sem=o_ss.at[slot], recv_sem=o_rs.at[slot],
            device_id=(me, other), device_id_type=MESH,
        )

    ins[1].wait()
    by_rows(0, yt)
    y_send = across(yt, yo, 0)
    y_send.start()
    ins[2].wait()
    by_rows(1, xt)
    x_send = across(xt.at[pl.ds(0, rows)], xo, 1)
    x_send.start()

    ins[3].wait()
    table = ritz[...].astype(F32)
    low = core == 0
    picked = jnp.where(low, table[:, :vecs], table[:, vecs:])
    picked = jnp.concatenate(
        [jnp.where(low, picked[:vecs], picked[vecs:]), jnp.where(low, picked[vecs:], picked[:vecs])],
        axis=0,
    )
    shift_r[...] = (-jnp.transpose(picked)).astype(BF16)
    picked = jnp.where(low, table[:vecs], table[vecs:])
    picked = jnp.concatenate(
        [
            jnp.where(low, picked[:, :vecs], picked[:, vecs:]),
            jnp.where(low, picked[:, vecs:], picked[:, :vecs]),
        ],
        axis=1,
    )
    shift_l[...] = (-picked).astype(BF16)
    summed[entries] = jnp.zeros((vecs, 128), F32)
    tab_copy.wait()

    x_backs = [
        pltpu.make_async_remote_copy(
            src_ref=x_out.at[n], dst_ref=x_in.at[BACK[n]],
            send_sem=x_ss.at[n], recv_sem=x_rs.at[BACK[n]],
            device_id=(near[n], core), device_id_type=MESH,
        )
        for n in range(3)
    ]

    rows_per = rows // CHUNKS

    def left_chunk(c, _):
        chunk_copy(c).wait()

        def left_row(i, _):
            r = c * rows_per + i
            use = [blk[r * SLOTS + s] for s in range(SLOTS)]
            prod = jnp.dot(yt[r], jnp.concatenate(use, axis=1), preferred_element_type=F32)
            for s in range(SLOTS):
                e = r * SLOTS + s
                summed[e] = prod[:, s * 128:(s + 1) * 128] + summed[tab_s[ROW_PREV + s, r]]
                blk[e] = use[s].T
            return 0

        lax.fori_loop(0, rows_per, left_row, 0, unroll=rows_per)

        @pl.when(c == CHUNKS // 2)
        def _():
            for n in range(3):
                asks[n].wait()
            copy = pltpu.make_async_copy(ask_in, ask_s, loc_sem.at[1])
            copy.start()
            copy.wait()
            for n in range(3):
                for t in range(2):
                    x_out[n, t] = xt[ask_s[n, t, 0]]
                x_backs[n].start()

        return 0

    lax.fori_loop(0, CHUNKS, left_chunk, 0)

    t_sends = []
    for n in range(3):
        two = jnp.broadcast_to(tab[ROW_TWO + n: ROW_TWO + n + 1, :], (vecs, 128)) > 0
        t_out[n, 0] = summed[tab_s[ROW_PICK + 2 * n, 0]].astype(BF16)
        t_out[n, 1] = jnp.where(two, summed[tab_s[ROW_PICK + 2 * n + 1, 0]], 0.0).astype(BF16)
        copy = pltpu.make_async_remote_copy(
            src_ref=t_out.at[n], dst_ref=t_in.at[BACK[n]],
            send_sem=t_ss.at[n], recv_sem=t_rs.at[BACK[n]],
            device_id=(near[n], core), device_id_type=MESH,
        )
        copy.start()
        t_sends.append(copy)

    lane = lax.broadcasted_iota(I32, (1, 128), 1)
    latest = jnp.full((1, 128), 6, I32)
    for u in range(6):
        latest = jnp.where(ask_in[u // 2, u % 2: u % 2 + 1, :] == lane, u, latest)
    lastc[0:1, :] = latest
    lastc_copy = pltpu.make_async_copy(lastc, lastc_s, loc_sem.at[2])
    lastc_copy.start()

    x_send.wait()
    for n in range(3):
        x_backs[n].wait()
    for n in range(3):
        for t in range(2):
            xt[rows + 2 * n + t] = x_in[n, t]

    def right_row(r, total):
        lhs = [xt[tab_s[ROW_EXT + s, r]] for s in range(SLOTS)] + [shift_r[...]]
        rhs = [blk[r * SLOTS + s] for s in range(SLOTS)] + [xt[r], xo[r]]
        res = jnp.dot(
            jnp.concatenate(lhs, axis=1), jnp.concatenate(rhs, axis=0), preferred_element_type=F32
        )
        right[pl.ds(r, vecs, stride=rows), :] = res
        return total + res * res

    acc[0:vecs] = lax.fori_loop(0, rows, right_row, jnp.zeros((vecs, 128), F32), unroll=8)
    right_out = pltpu.make_async_copy(right, right_hbm, out_sem.at[0])
    right_out.start()

    lastc_copy.wait()
    y_send.wait()
    back[6] = jnp.zeros((vecs, 128), F32)
    for n in range(3):
        t_sends[n].wait()
    for u in range(6):
        prev = jnp.int32(6)
        for v in range(u):
            prev = jnp.where(
                ask_s[v // 2, v % 2, 0] == ask_s[u // 2, u % 2, 0], jnp.int32(v), prev
            )
        back[u] = t_in[u // 2, u % 2].astype(F32) + back[prev]

    def left_res(c, total):
        rhs = jnp.concatenate([yt[c], yo[c]], axis=0)
        res = jnp.dot(shift_l[...], rhs, preferred_element_type=F32)
        res = res + summed[tab_s[ROW_LAST, c]] + back[lastc_s[0, c]]
        left[pl.ds(c, vecs, stride=rows), :] = res
        return total + res * res

    acc[vecs: 2 * vecs] = lax.fori_loop(0, rows, left_res, jnp.zeros((vecs, 128), F32), unroll=8)
    left_out = pltpu.make_async_copy(left, left_hbm, out_sem.at[1])
    left_out.start()

    mine = jnp.sum(jnp.transpose(acc[...]), axis=0, keepdims=True)
    mine = jnp.concatenate([mine, jnp.zeros((1, 128 - 2 * vecs), F32)], axis=1)
    for stage in range(3):
        parts[stage, side[stage]] = mine
        sends = []
        for turn in range(1, 4):
            copy = pltpu.make_async_remote_copy(
                src_ref=parts.at[stage, side[stage]],
                dst_ref=parts.at[stage, side[stage]],
                send_sem=n_ss.at[stage, turn], recv_sem=n_rs.at[stage, side[stage]],
                device_id=(partner(stage, turn), core), device_id_type=MESH,
            )
            copy.start()
            sends.append(copy)
        for turn in range(1, 4):
            sender = lax.rem(side[stage] + turn, 4)
            pltpu.make_async_remote_copy(
                src_ref=parts.at[stage, sender], dst_ref=parts.at[stage, sender],
                send_sem=n_ss.at[stage, turn], recv_sem=n_rs.at[stage, sender],
                device_id=(partner(stage, turn), core), device_id_type=MESH,
            ).wait_recv()
        for copy in sends:
            copy.wait_send()
        mine = parts[stage, 0] + parts[stage, 1] + parts[stage, 2] + parts[stage, 3]
    norm_ref[...] = mine
    right_out.wait()
    left_out.wait()


def shards(blocks, col_index, right_vecs, left_vecs, ritz):
    peers = lax.axis_size("rows")
    rows, slots = col_index.shape
    vecs, _, width = right_vecs.shape
    entries = rows * slots
    any_spec = pl.BlockSpec(memory_space=pl.ANY)
    dma = pltpu.SemaphoreType.DMA
    right, left, norms = pl.pallas_call(
        functools.partial(kernel, peers, rows, vecs),
        out_shape=(
            jax.ShapeDtypeStruct((vecs * rows, width), F32),
            jax.ShapeDtypeStruct((vecs * rows, width), F32),
            jax.ShapeDtypeStruct((1, 128), F32),
        ),
        in_specs=[any_spec] * 5,
        out_specs=(any_spec, any_spec, pl.BlockSpec(memory_space=pltpu.VMEM)),
        scratch_shapes=[
            pltpu.VMEM((slots, rows), I32),
            pltpu.VMEM((entries, width, width), BF16),
            pltpu.VMEM((2, vecs, rows, width), BF16),
            pltpu.VMEM((vecs * rows, width), F32),
            pltpu.VMEM((rows + 6, vecs, width), BF16),
            pltpu.VMEM((rows, vecs, width), BF16),
            pltpu.VMEM((rows, vecs, width), BF16),
            pltpu.VMEM((rows, vecs, width), BF16),
            pltpu.VMEM((entries + 1, vecs, width), F32),
            pltpu.VMEM((2 * vecs, 2 * vecs), BF16),
            pltpu.VMEM((vecs, 2 * vecs), BF16),
            pltpu.VMEM((vecs, 2 * vecs), BF16),
            pltpu.VMEM((32, 128), I32),
            pltpu.SMEM((32, 128), I32),
            pltpu.VMEM((3, 8, 128), I32),
            pltpu.VMEM((3, 8, 128), I32),
            pltpu.SMEM((3, 8, 128), I32),
            pltpu.VMEM((3, 2, vecs, width), BF16),
            pltpu.VMEM((3, 2, vecs, width), BF16),
            pltpu.VMEM((3, 2, vecs, width), BF16),
            pltpu.VMEM((3, 2, vecs, width), BF16),
            pltpu.VMEM((7, vecs, width), F32),
            pltpu.VMEM((8, 128), I32),
            pltpu.SMEM((8, 128), I32),
            pltpu.VMEM((vecs * rows, width), F32),
            pltpu.VMEM((vecs * rows, width), F32),
            pltpu.VMEM((2 * vecs, width), F32),
            pltpu.VMEM((3, 4, 1, 128), F32),
            dma((4,)),
            dma((CHUNKS,)),
            dma((3,)),
            dma((2,)),
            dma((3,)), dma((3,)),
            dma((3,)), dma((3,)),
            dma((3,)), dma((3,)),
            dma((2,)), dma((2,)),
            dma((3, 4)), dma((3, 4)),
        ],
        compiler_params=pltpu.CompilerParams(
            collective_id=0, has_side_effects=True, vmem_limit_bytes=48 << 20
        ),
    )(
        col_index.T,
        blocks.reshape(entries, width, width),
        right_vecs,
        left_vecs,
        ritz,
    )
    norms = jnp.sqrt(norms[0, : 2 * vecs])
    return (
        right.reshape(vecs, rows, width),
        left.reshape(vecs, rows, width),
        norms[:vecs],
        norms[vecs:],
    )


def solution(mesh):
    placed = (
        P("rows", None, None, None),
        P("rows", None),
        P("cols", "rows", None),
        P("cols", "rows", None),
        P(),
    )
    return jax.shard_map(
        shards,
        mesh=mesh,
        in_specs=placed,
        out_specs=(P("cols", "rows", None), P("cols", "rows", None), P("cols"), P("cols")),
        check_vma=False,
    )
```

time: 375 us -> 41.9 us (0.11)
  blocking collectives: 174 us -> 0 us
  other arithmetic: 71.6 us -> 0 us
  local copies, waits for them, and re-layouts: 46.6 us -> 6.01 us
  Pallas kernels: 0 us -> 34.9 us
  starting transfers between devices: 27.6 us -> 0 us
  matrix products: 25.3 us -> 0 us
  waiting for transfers between devices: 15.1 us -> 0 us
  between operations: 14.3 us -> 0.66 us
    psum x1 -> x0, blocking collectives: 174 us -> none  [shards(): lax.psum((jnp.sum(right_res * right_res, axis=(1, 2)), jnp.sum(left_res *...]
    scatter-add x2 -> x0, other arithmetic: 65.6 us -> none  [the longest x1 59.7 us: shards(): summed = jnp.zeros((vec_here, rows_here + peers * SENDS, width), jnp.floa...]
    pallas_call x0 -> x1, Pallas kernels: none -> 34.9 us  [shards(): pl.pallas_call(functools.partial(kernel, peers, rows, vecs), out_shape=(j...]
    all_to_all x3 -> x0, starting transfers between devices: 27.3 us -> none  [the longest x1 11.5 us: shards(): lax.all_to_all(wanted, 'rows', split_axis=0, concat_axis=0, tiled=True)]
    dot_general x4 -> x0, matrix products: 25.3 us -> none  [the longest x1 11.4 us: shards(): jnp.einsum('krsj,rsij->kri', gathered, blocks, preferred_element_type=jnp...]
    scatter x1 -> x0, local copies, waits for them, and re-layouts: 21.3 us -> none  [shards(): jnp.zeros((peers, SENDS), jnp.int32).at[target, rank]]
    all_to_all x3 -> x0, waiting for transfers between devices: 15 us -> none  [the longest x1 8.32 us: shards(): lax.all_to_all(summed[:, rows_here:, :].astype(jnp.bfloat16), 'rows', spl...]
    gather x3 -> x0, local copies, waits for them, and re-layouts: 10.2 us -> none  [the longest x2 6.84 us: shards(): outgoing = right_vecs[:, asked_flat, :]]
  transfers between devices with their start and end apart: 5 -> 0, of which waited for: 2 -> 0; matrix products, arithmetic and copies ran while one was open for 30% -> 0% of each run, Pallas kernels for 0% -> 0%
where the time goes in v1:
time: 41.9 us; the launch traced here: 41.6 us
  Pallas kernels  34.9 us (83%)
  local copies, waits for them, and re-layouts  6.01 us (14%)
  between operations  0.66 us (2%)
    pallas_call x1, Pallas kernels, shards(): pl.pallas_call(functools.partial(kernel, peers, rows, vecs), out_shape=(j...  34.9 us
    unnamed x10, local copies, waits for them, and re-layouts  5.42 us

profile of v1, /device:TPU:0, one launch (start us, length us, event | category | flops | bytes accessed | tf_op | source)
XLA Modules:
  0.0 41.6 jit_solution(2021000126535958135)
XLA Ops:
  0.6 0.0 copy-start
  0.6 1.0 %copy-done = bf16[32,64,128]{2,1,0:T(8,128)(2,1)S(1)} copy-done((bf16[32,64,128]{2,1,0:T(8,128)(2,1)S(1)}, bf16[32,64,128]{2,1,0:T(8,128)(2,1)}, u32[]{:S(2)}) %copy-start) | copy-done | bytes 524312
  1.7 0.0 copy-start.1
  1.7 1.0 %copy-done.1 = bf16[32,64,128]{2,1,0:T(8,128)(2,1)S(1)} copy-done((bf16[32,64,128]{2,1,0:T(8,128)(2,1)S(1)}, bf16[32,64,128]{2,1,0:T(8,128)(2,1)}, u32[]{:S(2)}) %copy-start.1) | copy-done | bytes 524312
  2.7 0.0 copy-start.2
  2.7 0.7 %copy-done.2 = bf16[64,64]{1,0:T(8,128)(2,1)S(1)} copy-done((bf16[64,64]{1,0:T(8,128)(2,1)S(1)}, bf16[64,64]{1,0:T(8,128)(2,1)}, u32[]{:S(2)}) %copy-start.2) | copy-done | bytes 8216
  3.4 0.0 copy-start.3
  3.4 0.7 %copy-done.3 = s32[64,7]{0,1:T(8,128)S(1)} copy-done((s32[64,7]{0,1:T(8,128)S(1)}, s32[64,7]{0,1:T(8,128)}, u32[]{:S(2)}) %copy-start.3) | copy-done | bytes 1816
  4.1 34.9 %shard_map.84 = (f32[2048,128]{1,0:T(8,128)S(1)}, f32[2048,128]{1,0:T(8,128)S(1)}, f32[1,128]{1,0:T(1,128)S(1)}) custom-call(s32[7,64]{1,0:T(8,128)S(1)} %bitcast.10, bf16[448,128,128]{2,1,0:T(8,128)(2,1)} %bitcast.11, bf16[32,64,128]{2,1,0:T(8,128)(2,1)S(1)} %copy-done, bf16[32,64,128]{2,1,0:T(8,128)(2,1)S(1)} %copy-done.1, bf16[64,64]{1,0:T(8,128)(2,1)S(1)} %copy-done.2), custom_call_target="tpu_custom_call" | custom-call | tf_op jit(solution)/shard_map/pallas_call | solution.py:338
  39.1 0.6 %slice_bitcast_fusion = (f32[32]{0:T(128)}, f32[32]{0:T(128)}) fusion(f32[1,64]{1,0:T(1,128)S(1)} %slice_sqrt_fusion), kind=kLoop, calls=%fused_computation | loop fusion | bytes 512 | tf_op jit(solution)/shard_map/slice | solution.py:401
  39.7 1.0 %copy.11 = f32[32,64,128]{2,1,0:T(8,128)} copy(f32[32,64,128]{2,1,0:T(8,128)S(1)} %bitcast.9) | data formatting | bytes 2097152
  40.6 1.0 %copy.12 = f32[32,64,128]{2,1,0:T(8,128)} copy(f32[32,64,128]{2,1,0:T(8,128)S(1)} %bitcast.8) | data formatting | bytes 2097152
  (1 shorter events, 0.0 us)
Async XLA Ops:
  0.6 1.0 %copy-start = (bf16[32,64,128]{2,1,0:T(8,128)(2,1)S(1)}, bf16[32,64,128]{2,1,0:T(8,128)(2,1)}, u32[]{:S(2)}) copy-start(bf16[32,64,128]{2,1,0:T(8,128)(2,1)} %x_hbm.1) | copy-start | bytes 1572868
  1.7 1.0 %copy-start.1 = (bf16[32,64,128]{2,1,0:T(8,128)(2,1)S(1)}, bf16[32,64,128]{2,1,0:T(8,128)(2,1)}, u32[]{:S(2)}) copy-start(bf16[32,64,128]{2,1,0:T(8,128)(2,1)} %y_hbm.1) | copy-start | bytes 1572868
  2.7 0.7 %copy-start.2 = (bf16[64,64]{1,0:T(8,128)(2,1)S(1)}, bf16[64,64]{1,0:T(8,128)(2,1)}, u32[]{:S(2)}) copy-start(bf16[64,64]{1,0:T(8,128)(2,1)} %ritz_hbm.1) | copy-start | bytes 24580
  3.4 0.7 %copy-start.3 = (s32[64,7]{0,1:T(8,128)S(1)}, s32[64,7]{0,1:T(8,128)}, u32[]{:S(2)}) copy-start(s32[64,7]{0,1:T(8,128)} %param.6) | copy-start | bytes 5380

commit v2 on v1

--- a/solution.py
+++ b/solution.py
@@ -13,7 +13,12 @@
 I32 = jnp.int32
 SLOTS = 7
 CHUNKS = 8
-ROW_EXT, ROW_PREV, ROW_LAST, ROW_PICK, ROW_TWO = 0, 8, 16, 17, 24
+PASSES = 4
+OFFSETS = sorted(
+    ((a, b, c) for a in range(4) for b in range(4) for c in range(4) if a + b + c),
+    key=lambda d: -sum(min(v, 4 - v) for v in d),
+)
+ROW_EXT, ROW_PREV, ROW_LAST, ROW_PICK, ROW_TWO, ROW_SAME, ROW_FIX = 0, 8, 16, 17, 24, 32, 38
 BACK = (1, 0, 2)
 
 
@@ -22,8 +27,8 @@
     cols_hbm, blocks_hbm, x_hbm, y_hbm, ritz_hbm,
     right_hbm, left_hbm, norm_ref,
     cols, blk, raw, wide, xt, yt, xo, yo, summed, ritz, shift_r, shift_l,
-    tab, tab_s, ask_out, ask_in, ask_s, x_out, x_in, t_out, t_in, back, lastc, lastc_s,
-    right, left, acc, parts,
+    tab, tab_s, ask_out, ask_in, ask_s, x_out, x_in, t_out, t_in, back, fixes, lastc, lastc_s,
+    kept, right, left, acc, parts,
     in_sem, blk_sem, loc_sem, out_sem,
     ask_ss, ask_rs, x_ss, x_rs, t_ss, t_rs, o_ss, o_rs, n_ss, n_rs,
 ):
@@ -39,10 +44,10 @@
     )
     other = 1 - core
     side = (me // 16, (me // 4) % 4, me % 4)
-    step = (16, 4, 1)
-
-    def partner(stage, turn):
-        return me + (lax.rem(side[stage] + turn, 4) - side[stage]) * step[stage]
+
+    def peer(offset):
+        at = [lax.rem(a + d, 4) for a, d in zip(side, offset)]
+        return at[0] * 16 + at[1] * 4 + at[2]
 
     ins = [
         pltpu.make_async_copy(cols_hbm, cols, in_sem.at[0]),
@@ -65,14 +70,9 @@
     lax.fori_loop(0, CHUNKS, start_chunk, 0)
 
     barrier = pltpu.get_barrier_semaphore()
-    for n in range(3):
-        pl.semaphore_signal(barrier, inc=1, device_id=(near[n], core), device_id_type=MESH)
     pl.semaphore_signal(barrier, inc=1, device_id=(me, other), device_id_type=MESH)
-    for stage in range(3):
-        for turn in range(1, 4):
-            pl.semaphore_signal(
-                barrier, inc=1, device_id=(partner(stage, turn), core), device_id_type=MESH
-            )
+    for offset in OFFSETS:
+        pl.semaphore_signal(barrier, inc=1, device_id=(peer(offset), core), device_id_type=MESH)
 
     ins[0].wait()
     col = cols[...]
@@ -88,25 +88,37 @@
     def all_max(v):
         return jnp.max(jnp.max(v, axis=1, keepdims=True), axis=0, keepdims=True)
 
-    ext = local
+    def put(row, value):
+        tab[row: row + 1, :] = jnp.broadcast_to(value, (1, 128))
+
+    lane = lax.broadcasted_iota(I32, (1, 128), 1)
+    tab[ROW_EXT: ROW_EXT + SLOTS, :rows] = jnp.where(owner == me, local, rows)
+    fix = jnp.full((1, 128), 6, I32)
+    pick_rows = []
     for n in range(3):
         here = owner == near[n]
         first = all_min(jnp.where(here, order, entries))
         final = all_max(jnp.where(here, order, 0))
-        id_first = all_max(jnp.where(order == first, local, 0))
-        id_final = all_max(jnp.where(order == final, local, 0))
-        ext = jnp.where(here, rows + 2 * n + (order == final).astype(I32), ext)
-        ask_out[n, 0:1, :] = jnp.broadcast_to(id_first, (1, 128))
-        ask_out[n, 1:2, :] = jnp.broadcast_to(id_final, (1, 128))
+        picks = (first, final)
+        for t in range(2):
+            hit = order == picks[t]
+            ask_out[n, t: t + 1, :] = jnp.broadcast_to(
+                all_max(jnp.where(hit, local, 0)), (1, 128)
+            )
+            put(ROW_PICK + 2 * n + t, jnp.minimum(picks[t], entries - 1))
+            at = all_max(jnp.where(hit, row_id, 0))
+            if t == 1:
+                at = jnp.where(first == final, -1, at)
+            same = jnp.full((1, 1), 6, I32)
+            for v, earlier in enumerate(pick_rows):
+                same = jnp.where(earlier == at, v, same)
+            put(ROW_SAME + 2 * n + t, same)
+            fix = jnp.where(lane == at, 2 * n + t, fix)
+            pick_rows.append(at)
         ask_out[n, 2:8, :] = jnp.zeros((6, 128), I32)
-        tab[ROW_PICK + 2 * n: ROW_PICK + 2 * n + 1, :] = jnp.broadcast_to(first, (1, 128))
-        tab[ROW_PICK + 2 * n + 1: ROW_PICK + 2 * n + 2, :] = jnp.broadcast_to(final, (1, 128))
-        tab[ROW_TWO + n: ROW_TWO + n + 1, :] = jnp.broadcast_to(
-            (first != final).astype(I32), (1, 128)
-        )
-    tab[ROW_EXT: ROW_EXT + SLOTS, :rows] = ext
-
-    pl.semaphore_wait(barrier, 13)
+        put(ROW_TWO + n, (first != final).astype(I32))
+    put(ROW_FIX, fix)
+
     asks = [
         pltpu.make_async_remote_copy(
             src_ref=ask_out.at[n], dst_ref=ask_in.at[BACK[n]],
@@ -115,8 +127,6 @@
         )
         for n in range(3)
     ]
-    for copy in asks:
-        copy.start()
 
     col_t = jnp.transpose(
         jnp.concatenate([col.astype(F32), jnp.full((1, rows), -1.0, F32)], axis=0)
@@ -165,11 +175,9 @@
     ins[1].wait()
     by_rows(0, yt)
     y_send = across(yt, yo, 0)
-    y_send.start()
     ins[2].wait()
     by_rows(1, xt)
     x_send = across(xt.at[pl.ds(0, rows)], xo, 1)
-    x_send.start()
 
     ins[3].wait()
     table = ritz[...].astype(F32)
@@ -190,7 +198,6 @@
     )
     shift_l[...] = (-picked).astype(BF16)
     summed[entries] = jnp.zeros((vecs, 128), F32)
-    tab_copy.wait()
 
     x_backs = [
         pltpu.make_async_remote_copy(
@@ -201,38 +208,63 @@
         for n in range(3)
     ]
 
-    rows_per = rows // CHUNKS
-
-    def left_chunk(c, _):
-        chunk_copy(c).wait()
-
-        def left_row(i, _):
-            r = c * rows_per + i
-            use = [blk[r * SLOTS + s] for s in range(SLOTS)]
-            prod = jnp.dot(yt[r], jnp.concatenate(use, axis=1), preferred_element_type=F32)
-            for s in range(SLOTS):
-                e = r * SLOTS + s
-                summed[e] = prod[:, s * 128:(s + 1) * 128] + summed[tab_s[ROW_PREV + s, r]]
-                blk[e] = use[s].T
-            return 0
-
-        lax.fori_loop(0, rows_per, left_row, 0, unroll=rows_per)
-
-        @pl.when(c == CHUNKS // 2)
+    xt[rows] = jnp.zeros((vecs, 128), BF16)
+    pl.semaphore_wait(barrier, peers)
+    for copy in asks:
+        copy.start()
+    y_send.start()
+    x_send.start()
+    tab_copy.wait()
+
+    per_pass = rows // PASSES
+
+    ask_copy = pltpu.make_async_copy(ask_in, ask_s, loc_sem.at[1])
+    lastc_copy = pltpu.make_async_copy(lastc, lastc_s, loc_sem.at[2])
+
+    def one_pass(c, _):
+        for half_pass in range(CHUNKS // PASSES):
+            chunk_copy(c * (CHUNKS // PASSES) + half_pass).wait()
+
+        @pl.when(c == 2)
         def _():
             for n in range(3):
                 asks[n].wait()
-            copy = pltpu.make_async_copy(ask_in, ask_s, loc_sem.at[1])
-            copy.start()
-            copy.wait()
+            ask_copy.start()
+            latest = jnp.full((1, 128), 6, I32)
+            for u in range(6):
+                latest = jnp.where(ask_in[u // 2, u % 2: u % 2 + 1, :] == lane, u, latest)
+            lastc[0:1, :] = latest
+            lastc_copy.start()
+
+        @pl.when(c == 3)
+        def _():
+            ask_copy.wait()
+            lastc_copy.wait()
             for n in range(3):
                 for t in range(2):
                     x_out[n, t] = xt[ask_s[n, t, 0]]
                 x_backs[n].start()
 
+        def both(i, _):
+            r = c * per_pass + i
+            use = [blk[r * SLOTS + s] for s in range(SLOTS)]
+            prod = jnp.dot(yt[r], jnp.concatenate(use, axis=1), preferred_element_type=F32)
+            lhs = [xt[tab_s[ROW_EXT + s, r]] for s in range(SLOTS)]
+            kept[r] = jnp.dot(
+                jnp.concatenate(lhs, axis=1),
+                jnp.concatenate([block.T for block in use], axis=0),
+                preferred_element_type=F32,
+            )
+            for s in range(SLOTS):
+                summed[r * SLOTS + s] = (
+                    prod[:, s * 128:(s + 1) * 128] + summed[tab_s[ROW_PREV + s, r]]
+                )
+            return 0
+
+        lax.fori_loop(0, per_pass, both, 0, unroll=True)
         return 0
 
-    lax.fori_loop(0, CHUNKS, left_chunk, 0)
+    lax.fori_loop(0, PASSES, one_pass, 0)
 
     t_sends = []
     for n in range(3):
@@ -247,27 +279,22 @@
         copy.start()
         t_sends.append(copy)
 
-    lane = lax.broadcasted_iota(I32, (1, 128), 1)
-    latest = jnp.full((1, 128), 6, I32)
-    for u in range(6):
-        latest = jnp.where(ask_in[u // 2, u % 2: u % 2 + 1, :] == lane, u, latest)
-    lastc[0:1, :] = latest
-    lastc_copy = pltpu.make_async_copy(lastc, lastc_s, loc_sem.at[2])
-    lastc_copy.start()
-
-    x_send.wait()
     for n in range(3):
         x_backs[n].wait()
-    for n in range(3):
-        for t in range(2):
-            xt[rows + 2 * n + t] = x_in[n, t]
+    fixes[6] = jnp.zeros((vecs, 128), F32)
+    for u in range(6):
+        fixes[u] = lax.dot_general(
+            x_in[u // 2, u % 2], blk[tab_s[ROW_PICK + u, 0]], (((1,), (1,)), ((), ())),
+            preferred_element_type=F32,
+        ) + fixes[tab_s[ROW_SAME + u, 0]]
+    x_send.wait()
+    y_send.wait()
 
     def right_row(r, total):
-        lhs = [xt[tab_s[ROW_EXT + s, r]] for s in range(SLOTS)] + [shift_r[...]]
-        rhs = [blk[r * SLOTS + s] for s in range(SLOTS)] + [xt[r], xo[r]]
         res = jnp.dot(
-            jnp.concatenate(lhs, axis=1), jnp.concatenate(rhs, axis=0), preferred_element_type=F32
-        )
+            shift_r[...], jnp.concatenate([xt[r], xo[r]], axis=0), preferred_element_type=F32
+        )
+        res = res + kept[r] + fixes[tab_s[ROW_FIX, r]]
         right[pl.ds(r, vecs, stride=rows), :] = res
         return total + res * res
 
@@ -275,8 +302,6 @@
     right_out = pltpu.make_async_copy(right, right_hbm, out_sem.at[0])
     right_out.start()
 
-    lastc_copy.wait()
-    y_send.wait()
     back[6] = jnp.zeros((vecs, 128), F32)
     for n in range(3):
         t_sends[n].wait()
@@ -289,8 +314,9 @@
         back[u] = t_in[u // 2, u % 2].astype(F32) + back[prev]
 
     def left_res(c, total):
-        rhs = jnp.concatenate([yt[c], yo[c]], axis=0)
-        res = jnp.dot(shift_l[...], rhs, preferred_element_type=F32)
+        res = jnp.dot(
+            shift_l[...], jnp.concatenate([yt[c], yo[c]], axis=0), preferred_element_type=F32
+        )
         res = res + summed[tab_s[ROW_LAST, c]] + back[lastc_s[0, c]]
         left[pl.ds(c, vecs, stride=rows), :] = res
         return total + res * res
@@ -301,29 +327,24 @@
 
     mine = jnp.sum(jnp.transpose(acc[...]), axis=0, keepdims=True)
     mine = jnp.concatenate([mine, jnp.zeros((1, 128 - 2 * vecs), F32)], axis=1)
-    for stage in range(3):
-        parts[stage, side[stage]] = mine
-        sends = []
-        for turn in range(1, 4):
-            copy = pltpu.make_async_remote_copy(
-                src_ref=parts.at[stage, side[stage]],
-                dst_ref=parts.at[stage, side[stage]],
-                send_sem=n_ss.at[stage, turn], recv_sem=n_rs.at[stage, side[stage]],
-                device_id=(partner(stage, turn), core), device_id_type=MESH,
-            )
-            copy.start()
-            sends.append(copy)
-        for turn in range(1, 4):
-            sender = lax.rem(side[stage] + turn, 4)
-            pltpu.make_async_remote_copy(
-                src_ref=parts.at[stage, sender], dst_ref=parts.at[stage, sender],
-                send_sem=n_ss.at[stage, turn], recv_sem=n_rs.at[stage, sender],
-                device_id=(partner(stage, turn), core), device_id_type=MESH,
-            ).wait_recv()
-        for copy in sends:
-            copy.wait_send()
-        mine = parts[stage, 0] + parts[stage, 1] + parts[stage, 2] + parts[stage, 3]
-    norm_ref[...] = mine
+    parts[me] = mine
+
+    def share(to):
+        return pltpu.make_async_remote_copy(
+            src_ref=parts.at[me], dst_ref=parts.at[me], send_sem=n_ss.at[0], recv_sem=n_rs.at[0],
+            device_id=(to, core), device_id_type=MESH,
+        )
+
+    for offset in OFFSETS:
+        share(peer(offset)).start()
+    every = pltpu.make_async_remote_copy(
+        src_ref=parts.at[pl.ds(0, peers - 1)], dst_ref=parts.at[pl.ds(0, peers - 1)],
+        send_sem=n_ss.at[0], recv_sem=n_rs.at[0],
+        device_id=(near[0], core), device_id_type=MESH,
+    )
+    every.wait_recv()
+    every.wait_send()
+    norm_ref[...] = jnp.sqrt(jnp.sum(parts[...], axis=0))
     right_out.wait()
     left_out.wait()
 
@@ -349,7 +370,7 @@
             pltpu.VMEM((entries, width, width), BF16),
             pltpu.VMEM((2, vecs, rows, width), BF16),
             pltpu.VMEM((vecs * rows, width), F32),
-            pltpu.VMEM((rows + 6, vecs, width), BF16),
+            pltpu.VMEM((rows + 1, vecs, width), BF16),
             pltpu.VMEM((rows, vecs, width), BF16),
             pltpu.VMEM((rows, vecs, width), BF16),
             pltpu.VMEM((rows, vecs, width), BF16),
@@ -357,8 +378,8 @@
             pltpu.VMEM((2 * vecs, 2 * vecs), BF16),
             pltpu.VMEM((vecs, 2 * vecs), BF16),
             pltpu.VMEM((vecs, 2 * vecs), BF16),
-            pltpu.VMEM((32, 128), I32),
-            pltpu.SMEM((32, 128), I32),
+            pltpu.VMEM((40, 128), I32),
+            pltpu.SMEM((40, 128), I32),
             pltpu.VMEM((3, 8, 128), I32),
             pltpu.VMEM((3, 8, 128), I32),
             pltpu.SMEM((3, 8, 128), I32),
@@ -367,12 +388,14 @@
             pltpu.VMEM((3, 2, vecs, width), BF16),
             pltpu.VMEM((3, 2, vecs, width), BF16),
             pltpu.VMEM((7, vecs, width), F32),
+            pltpu.VMEM((7, vecs, width), F32),
             pltpu.VMEM((8, 128), I32),
             pltpu.SMEM((8, 128), I32),
+            pltpu.VMEM((rows, vecs, width), F32),
             pltpu.VMEM((vecs * rows, width), F32),
             pltpu.VMEM((vecs * rows, width), F32),
             pltpu.VMEM((2 * vecs, width), F32),
-            pltpu.VMEM((3, 4, 1, 128), F32),
+            pltpu.VMEM((peers, 1, 128), F32),
             dma((4,)),
             dma((CHUNKS,)),
             dma((3,)),
@@ -381,10 +404,10 @@
             dma((3,)), dma((3,)),
             dma((3,)), dma((3,)),
             dma((2,)), dma((2,)),
-            dma((3, 4)), dma((3, 4)),
+            dma((1,)), dma((1,)),
         ],
         compiler_params=pltpu.CompilerParams(
-            collective_id=0, has_side_effects=True, vmem_limit_bytes=48 << 20
+            collective_id=0, has_side_effects=True, vmem_limit_bytes=63 << 20
         ),
     )(
         col_index.T,
@@ -393,7 +416,7 @@
         left_vecs,
         ritz,
     )
-    norms = jnp.sqrt(norms[0, : 2 * vecs])
+    norms = norms[0, : 2 * vecs]
     return (
         right.reshape(vecs, rows, width),
         left.reshape(vecs, rows, width),

time: 41.9 us -> 36.3 us (0.87)
  Pallas kernels: 34.9 us -> 29.6 us
    pallas_call x1, Pallas kernels: 34.9 us -> 29.6 us  [shards(): pl.pallas_call(functools.partial(kernel, peers, rows, vecs), out_shape=(j...]
    unnamed x10 -> x2, local copies, waits for them, and re-layouts: 5.42 us -> 4.61 us
    slice x1, local copies, waits for them, and re-layouts: 0.58 us -> 1.27 us  [shards(): norms[vecs:]]
where the time goes in v2:
time: 36.3 us; the launch traced here: 36.1 us
  Pallas kernels  29.6 us (82%)
  local copies, waits for them, and re-layouts  5.88 us (16%)
  between operations  0.64 us (2%)
    pallas_call x1, Pallas kernels, shards(): pl.pallas_call(functools.partial(kernel, peers, rows, vecs), out_shape=(j...  29.6 us
    unnamed x2, local copies, waits for them, and re-layouts  4.61 us
    slice x1, local copies, waits for them, and re-layouts, shards(): norms[vecs:]  1.27 us

profile of v2, /device:TPU:0, one launch (start us, length us, event | category | flops | bytes accessed | tf_op | source)
XLA Modules:
  0.0 36.1 jit_solution(10243456264437043873)
XLA Ops:
  0.6 29.6 %shard_map.84 = (f32[2048,128]{1,0:T(8,128)}, f32[2048,128]{1,0:T(8,128)}, f32[1,128]{1,0:T(1,128)}) custom-call(s32[7,64]{1,0:T(8,128)} %bitcast.11, bf16[448,128,128]{2,1,0:T(8,128)(2,1)} %bitcast.8, bf16[32,64,128]{2,1,0:T(8,128)(2,1)} %x_hbm.1, bf16[32,64,128]{2,1,0:T(8,128)(2,1)} %y_hbm.1, bf16[64,64]{1,0:T(8,128)(2,1)} %ritz_hbm.1), custom_call_target="tpu_custom_call" | custom-call | tf_op jit(solution)/shard_map/pallas_call | solution.py:359
  30.3 1.3 %slice_bitcast_fusion = (f32[32]{0:T(128)}, f32[32]{0:T(128)}) fusion(f32[1,128]{1,0:T(1,128)} %get-tuple-element.9), kind=kLoop, calls=%fused_computation | loop fusion | bytes 512 | tf_op jit(solution)/shard_map/slice | solution.py:424
  31.5 2.3 %copy.11 = f32[32,64,128]{2,1,0:T(8,128)} copy(f32[32,64,128]{2,1,0:T(8,128)} %bitcast.10) | data formatting | bytes 2097152
  33.8 2.3 %copy.12 = f32[32,64,128]{2,1,0:T(8,128)} copy(f32[32,64,128]{2,1,0:T(8,128)} %bitcast.9) | data formatting | bytes 2097152

commit v3 on v2

--- a/solution.py
+++ b/solution.py
@@ -18,7 +18,7 @@
     ((a, b, c) for a in range(4) for b in range(4) for c in range(4) if a + b + c),
     key=lambda d: -sum(min(v, 4 - v) for v in d),
 )
-ROW_EXT, ROW_PREV, ROW_LAST, ROW_PICK, ROW_TWO, ROW_SAME, ROW_FIX = 0, 8, 16, 17, 24, 32, 38
+ROW_EXT, ROW_PREV, ROW_LAST, ROW_PICK, ROW_TWO, ROW_SAME, ROW_FIX, ROW_AT = 0, 8, 16, 17, 24, 32, 38, 40
 BACK = (1, 0, 2)
 
 
@@ -28,9 +28,9 @@
     right_hbm, left_hbm, norm_ref,
     cols, blk, raw, wide, xt, yt, xo, yo, summed, ritz, shift_r, shift_l,
     tab, tab_s, ask_out, ask_in, ask_s, x_out, x_in, t_out, t_in, back, fixes, lastc, lastc_s,
-    kept, right, left, acc, parts,
+    kept, kept_l, acc, parts,
     in_sem, blk_sem, loc_sem, out_sem,
-    ask_ss, ask_rs, x_ss, x_rs, t_ss, t_rs, o_ss, o_rs, n_ss, n_rs,
+    ask_ss, ask_rs, x_ss, x_rs, t_ss, t_rs, o_ss, o_rs, n_ss, n_rs, all_x, all_z,
 ):
     me = lax.axis_index("rows")
     core = lax.axis_index("cols")
@@ -70,9 +70,14 @@
     lax.fori_loop(0, CHUNKS, start_chunk, 0)
 
     barrier = pltpu.get_barrier_semaphore()
+    lines = [
+        [peer(tuple(d if a == axis else 0 for a in range(3))) for d in range(1, 4)]
+        for axis in range(3)
+    ]
+    met = list(near) + lines[0] + lines[1] + lines[2]
     pl.semaphore_signal(barrier, inc=1, device_id=(me, other), device_id_type=MESH)
-    for offset in OFFSETS:
-        pl.semaphore_signal(barrier, inc=1, device_id=(peer(offset), core), device_id_type=MESH)
+    for to in met:
+        pl.semaphore_signal(barrier, inc=1, device_id=(to, core), device_id_type=MESH)
 
     ins[0].wait()
     col = cols[...]
@@ -107,6 +112,7 @@
             )
             put(ROW_PICK + 2 * n + t, jnp.minimum(picks[t], entries - 1))
             at = all_max(jnp.where(hit, row_id, 0))
+            put(ROW_AT + 2 * n + t, at)
             if t == 1:
                 at = jnp.where(first == final, -1, at)
             same = jnp.full((1, 1), 6, I32)
@@ -119,6 +125,7 @@
         put(ROW_TWO + n, (first != final).astype(I32))
     put(ROW_FIX, fix)
 
+    pl.semaphore_wait(barrier, len(met) + 1)
     asks = [
         pltpu.make_async_remote_copy(
             src_ref=ask_out.at[n], dst_ref=ask_in.at[BACK[n]],
@@ -127,6 +134,11 @@
         )
         for n in range(3)
     ]
+
+    for copy in asks:
+        copy.start()
+    for to in lines[0]:
+        pl.semaphore_signal(all_x, inc=1, device_id=(to, core), device_id_type=MESH)
 
     col_t = jnp.transpose(
         jnp.concatenate([col.astype(F32), jnp.full((1, rows), -1.0, F32)], axis=0)
@@ -175,9 +187,11 @@
     ins[1].wait()
     by_rows(0, yt)
     y_send = across(yt, yo, 0)
+    y_send.start()
     ins[2].wait()
     by_rows(1, xt)
     x_send = across(xt.at[pl.ds(0, rows)], xo, 1)
+    x_send.start()
 
     ins[3].wait()
     table = ritz[...].astype(F32)
@@ -209,23 +223,26 @@
     ]
 
     xt[rows] = jnp.zeros((vecs, 128), BF16)
-    pl.semaphore_wait(barrier, peers)
-    for copy in asks:
-        copy.start()
-    y_send.start()
-    x_send.start()
     tab_copy.wait()
 
     per_pass = rows // PASSES
 
     ask_copy = pltpu.make_async_copy(ask_in, ask_s, loc_sem.at[1])
     lastc_copy = pltpu.make_async_copy(lastc, lastc_s, loc_sem.at[2])
+    t_sends = [
+        pltpu.make_async_remote_copy(
+            src_ref=t_out.at[n], dst_ref=t_in.at[BACK[n]],
+            send_sem=t_ss.at[n], recv_sem=t_rs.at[BACK[n]],
+            device_id=(near[n], core), device_id_type=MESH,
+        )
+        for n in range(3)
+    ]
 
     def one_pass(c, _):
         for half_pass in range(CHUNKS // PASSES):
             chunk_copy(c * (CHUNKS // PASSES) + half_pass).wait()
 
-        @pl.when(c == 2)
+        @pl.when(c == PASSES - 1)
         def _():
             for n in range(3):
                 asks[n].wait()
@@ -235,15 +252,27 @@
                 latest = jnp.where(ask_in[u // 2, u % 2: u % 2 + 1, :] == lane, u, latest)
             lastc[0:1, :] = latest
             lastc_copy.start()
-
-        @pl.when(c == 3)
-        def _():
+            for n in range(3):
+                two = jnp.broadcast_to(tab[ROW_TWO + n: ROW_TWO + n + 1, :], (vecs, 128)) > 0
+                sums = [
+                    jnp.dot(
+                        yt[tab_s[ROW_AT + 2 * n + t, 0]], blk[tab_s[ROW_PICK + 2 * n + t, 0]],
+                        preferred_element_type=F32,
+                    )
+                    for t in range(2)
+                ]
+                t_out[n, 0] = sums[0].astype(BF16)
+                t_out[n, 1] = jnp.where(two, sums[1], 0.0).astype(BF16)
             ask_copy.wait()
-            lastc_copy.wait()
             for n in range(3):
                 for t in range(2):
                     x_out[n, t] = xt[ask_s[n, t, 0]]
                 x_backs[n].start()
+            for n in range(3):
+                t_sends[n].start()
+            pl.semaphore_wait(all_x, 3)
+            for to in lines[1]:
+                pl.semaphore_signal(all_z, inc=1, device_id=(to, core), device_id_type=MESH)
 
         def both(i, _):
             r = c * per_pass + i
@@ -266,18 +295,19 @@
 
     lax.fori_loop(0, PASSES, one_pass, 0)
 
-    t_sends = []
-    for n in range(3):
-        two = jnp.broadcast_to(tab[ROW_TWO + n: ROW_TWO + n + 1, :], (vecs, 128)) > 0
-        t_out[n, 0] = summed[tab_s[ROW_PICK + 2 * n, 0]].astype(BF16)
-        t_out[n, 1] = jnp.where(two, summed[tab_s[ROW_PICK + 2 * n + 1, 0]], 0.0).astype(BF16)
-        copy = pltpu.make_async_remote_copy(
-            src_ref=t_out.at[n], dst_ref=t_in.at[BACK[n]],
-            send_sem=t_ss.at[n], recv_sem=t_rs.at[BACK[n]],
-            device_id=(near[n], core), device_id_type=MESH,
-        )
-        copy.start()
-        t_sends.append(copy)
+    x_send.wait()
+    y_send.wait()
+
+    def shifts(r, _):
+        kept[r] += jnp.dot(
+            shift_r[...], jnp.concatenate([xt[r], xo[r]], axis=0), preferred_element_type=F32
+        )
+        kept_l[r] = summed[tab_s[ROW_LAST, r]] + jnp.dot(
+            shift_l[...], jnp.concatenate([yt[r], yo[r]], axis=0), preferred_element_type=F32
+        )
+        return 0
+
+    lax.fori_loop(0, rows, shifts, 0, unroll=8)
 
     for n in range(3):
         x_backs[n].wait()
@@ -287,21 +317,16 @@
             x_in[u // 2, u % 2], blk[tab_s[ROW_PICK + u, 0]], (((1,), (1,)), ((), ())),
             preferred_element_type=F32,
         ) + fixes[tab_s[ROW_SAME + u, 0]]
-    x_send.wait()
-    y_send.wait()
-
-    def right_row(r, total):
-        res = jnp.dot(
-            shift_r[...], jnp.concatenate([xt[r], xo[r]], axis=0), preferred_element_type=F32
-        )
-        res = res + kept[r] + fixes[tab_s[ROW_FIX, r]]
-        right[pl.ds(r, vecs, stride=rows), :] = res
+    def right_res(r, total):
+        res = kept[r] + fixes[tab_s[ROW_FIX, r]]
+        kept[r] = res
         return total + res * res
 
-    acc[0:vecs] = lax.fori_loop(0, rows, right_row, jnp.zeros((vecs, 128), F32), unroll=8)
-    right_out = pltpu.make_async_copy(right, right_hbm, out_sem.at[0])
+    acc[0:vecs] = lax.fori_loop(0, rows, right_res, jnp.zeros((vecs, 128), F32), unroll=8)
+    right_out = pltpu.make_async_copy(kept, right_hbm, out_sem.at[0])
     right_out.start()
 
+    lastc_copy.wait()
     back[6] = jnp.zeros((vecs, 128), F32)
     for n in range(3):
         t_sends[n].wait()
@@ -314,15 +339,12 @@
         back[u] = t_in[u // 2, u % 2].astype(F32) + back[prev]
 
     def left_res(c, total):
-        res = jnp.dot(
-            shift_l[...], jnp.concatenate([yt[c], yo[c]], axis=0), preferred_element_type=F32
-        )
-        res = res + summed[tab_s[ROW_LAST, c]] + back[lastc_s[0, c]]
-        left[pl.ds(c, vecs, stride=rows), :] = res
+        res = kept_l[c] + back[lastc_s[0, c]]
+        kept_l[c] = res
         return total + res * res
 
     acc[vecs: 2 * vecs] = lax.fori_loop(0, rows, left_res, jnp.zeros((vecs, 128), F32), unroll=8)
-    left_out = pltpu.make_async_copy(left, left_hbm, out_sem.at[1])
+    left_out = pltpu.make_async_copy(kept_l, left_hbm, out_sem.at[1])
     left_out.start()
 
     mine = jnp.sum(jnp.transpose(acc[...]), axis=0, keepdims=True)
@@ -335,6 +357,7 @@
             device_id=(to, core), device_id_type=MESH,
         )
 
+    pl.semaphore_wait(all_z, 3)
     for offset in OFFSETS:
         share(peer(offset)).start()
     every = pltpu.make_async_remote_copy(
@@ -359,8 +382,8 @@
     right, left, norms = pl.pallas_call(
         functools.partial(kernel, peers, rows, vecs),
         out_shape=(
-            jax.ShapeDtypeStruct((vecs * rows, width), F32),
-            jax.ShapeDtypeStruct((vecs * rows, width), F32),
+            jax.ShapeDtypeStruct((rows, vecs, width), F32),
+            jax.ShapeDtypeStruct((rows, vecs, width), F32),
             jax.ShapeDtypeStruct((1, 128), F32),
         ),
         in_specs=[any_spec] * 5,
@@ -378,8 +401,8 @@
             pltpu.VMEM((2 * vecs, 2 * vecs), BF16),
             pltpu.VMEM((vecs, 2 * vecs), BF16),
             pltpu.VMEM((vecs, 2 * vecs), BF16),
-            pltpu.VMEM((40, 128), I32),
-            pltpu.SMEM((40, 128), I32),
+            pltpu.VMEM((48, 128), I32),
+            pltpu.SMEM((48, 128), I32),
             pltpu.VMEM((3, 8, 128), I32),
             pltpu.VMEM((3, 8, 128), I32),
             pltpu.SMEM((3, 8, 128), I32),
@@ -392,8 +415,7 @@
             pltpu.VMEM((8, 128), I32),
             pltpu.SMEM((8, 128), I32),
             pltpu.VMEM((rows, vecs, width), F32),
-            pltpu.VMEM((vecs * rows, width), F32),
-            pltpu.VMEM((vecs * rows, width), F32),
+            pltpu.VMEM((rows, vecs, width), F32),
             pltpu.VMEM((2 * vecs, width), F32),
             pltpu.VMEM((peers, 1, 128), F32),
             dma((4,)),
@@ -405,21 +427,27 @@
             dma((3,)), dma((3,)),
             dma((2,)), dma((2,)),
             dma((1,)), dma((1,)),
+            pltpu.SemaphoreType.REGULAR, pltpu.SemaphoreType.REGULAR,
         ],
         compiler_params=pltpu.CompilerParams(
-            collective_id=0, has_side_effects=True, vmem_limit_bytes=63 << 20
+            collective_id=0, has_side_effects=True, vmem_limit_bytes=44 << 20
         ),
     )(
-        col_index.T,
-        blocks.reshape(entries, width, width),
-        right_vecs,
-        left_vecs,
-        ritz,
+        *(
+            pltpu.with_memory_space_constraint(arg, pltpu.HBM)
+            for arg in (
+                col_index.T,
+                blocks.reshape(entries, width, width),
+                right_vecs,
+                left_vecs,
+                ritz,
+            )
+        )
     )
     norms = norms[0, : 2 * vecs]
     return (
-        right.reshape(vecs, rows, width),
-        left.reshape(vecs, rows, width),
+        jnp.swapaxes(right, 0, 1),
+        jnp.swapaxes(left, 0, 1),
         norms[:vecs],
         norms[vecs:],
     )

time: 36.3 us -> 31.3 us (0.86)
  Pallas kernels: 29.6 us -> 26.8 us
  local copies, waits for them, and re-layouts: 5.88 us -> 3.74 us
    pallas_call x1, Pallas kernels: 29.6 us -> 26.8 us  [shards(): pl.pallas_call(functools.partial(kernel, peers, rows, vecs), out_shape=(j...]
    unnamed x2, local copies, waits for them, and re-layouts: 4.61 us -> 3.16 us
    slice x1, local copies, waits for them, and re-layouts: 1.27 us -> 0.58 us  [shards(): norms[vecs:]]
where the time goes in v3:
time: 31.3 us; the launch traced here: 31.2 us
  Pallas kernels  26.8 us (86%)
  local copies, waits for them, and re-layouts  3.74 us (12%)
  between operations  0.64 us (2%)
    pallas_call x1, Pallas kernels, shards(): pl.pallas_call(functools.partial(kernel, peers, rows, vecs), out_shape=(j...  26.8 us
    unnamed x2, local copies, waits for them, and re-layouts  3.16 us

profile of v3, /device:TPU:0, one launch (start us, length us, event | category | flops | bytes accessed | tf_op | source)
XLA Modules:
  0.0 31.2 jit_solution(12149390871802414124)
XLA Ops:
  0.6 26.8 %shard_map.84 = (f32[64,32,128]{2,1,0:T(8,128)S(1)}, f32[64,32,128]{2,1,0:T(8,128)S(1)}, f32[1,128]{1,0:T(1,128)S(1)}) custom-call(s32[7,64]{1,0:T(8,128)} %bitcast.11, bf16[448,128,128]{2,1,0:T(8,128)(2,1)} %bitcast.10, bf16[32,64,128]{2,1,0:T(8,128)(2,1)} %x_hbm.1, bf16[32,64,128]{2,1,0:T(8,128)(2,1)} %y_hbm.1, bf16[64,64]{1,0:T(8,128)(2,1)} %ritz_hbm.1), custom_call_target="tpu_custom_call" | custom-call | tf_op jit(solution)/shard_map/pallas_call | solution.py:382
  27.5 1.6 %copy.9 = f32[32,64,128]{2,1,0:T(8,128)} copy(f32[32,64,128]{2,0,1:T(8,128)S(1)} %bitcast.9) | data formatting | bytes 2097152
  29.1 1.6 %copy.10 = f32[32,64,128]{2,1,0:T(8,128)} copy(f32[32,64,128]{2,0,1:T(8,128)S(1)} %bitcast.8) | data formatting | bytes 2097152
  30.6 0.6 %slice_bitcast_fusion = (f32[32]{0:T(128)}, f32[32]{0:T(128)}) fusion(f32[1,128]{1,0:T(1,128)S(1)} %get-tuple-element.9), kind=kLoop, calls=%fused_computation | loop fusion | bytes 512 | tf_op jit(solution)/shard_map/slice | solution.py:452

commit v4 on v3

--- a/solution.py
+++ b/solution.py
@@ -49,6 +49,16 @@
         at = [lax.rem(a + d, 4) for a, d in zip(side, offset)]
         return at[0] * 16 + at[1] * 4 + at[2]
 
+    barrier = pltpu.get_barrier_semaphore()
+    lines = [
+        [peer(tuple(d if a == axis else 0 for a in range(3))) for d in range(1, 4)]
+        for axis in range(3)
+    ]
+    met = list(near) + lines[0] + lines[1] + lines[2]
+    pl.semaphore_signal(barrier, inc=1, device_id=(me, other), device_id_type=MESH)
+    for to in met:
+        pl.semaphore_signal(barrier, inc=1, device_id=(to, core), device_id_type=MESH)
+
     ins = [
         pltpu.make_async_copy(cols_hbm, cols, in_sem.at[0]),
         pltpu.make_async_copy(y_hbm, raw.at[0], in_sem.at[1]),
@@ -68,16 +78,6 @@
         return 0
 
     lax.fori_loop(0, CHUNKS, start_chunk, 0)
-
-    barrier = pltpu.get_barrier_semaphore()
-    lines = [
-        [peer(tuple(d if a == axis else 0 for a in range(3))) for d in range(1, 4)]
-        for axis in range(3)
-    ]
-    met = list(near) + lines[0] + lines[1] + lines[2]
-    pl.semaphore_signal(barrier, inc=1, device_id=(me, other), device_id_type=MESH)
-    for to in met:
-        pl.semaphore_signal(barrier, inc=1, device_id=(to, core), device_id_type=MESH)
 
     ins[0].wait()
     col = cols[...]
@@ -125,7 +125,6 @@
         put(ROW_TWO + n, (first != final).astype(I32))
     put(ROW_FIX, fix)
 
-    pl.semaphore_wait(barrier, len(met) + 1)
     asks = [
         pltpu.make_async_remote_copy(
             src_ref=ask_out.at[n], dst_ref=ask_in.at[BACK[n]],
@@ -134,11 +133,6 @@
         )
         for n in range(3)
     ]
-
-    for copy in asks:
-        copy.start()
-    for to in lines[0]:
-        pl.semaphore_signal(all_x, inc=1, device_id=(to, core), device_id_type=MESH)
 
     col_t = jnp.transpose(
         jnp.concatenate([col.astype(F32), jnp.full((1, rows), -1.0, F32)], axis=0)
@@ -187,6 +181,11 @@
     ins[1].wait()
     by_rows(0, yt)
     y_send = across(yt, yo, 0)
+    pl.semaphore_wait(barrier, len(met) + 1)
+    for copy in asks:
+        copy.start()
+    for to in lines[0]:
+        pl.semaphore_signal(all_x, inc=1, device_id=(to, core), device_id_type=MESH)
     y_send.start()
     ins[2].wait()
     by_rows(1, xt)
@@ -244,14 +243,6 @@
 
         @pl.when(c == PASSES - 1)
         def _():
-            for n in range(3):
-                asks[n].wait()
-            ask_copy.start()
-            latest = jnp.full((1, 128), 6, I32)
-            for u in range(6):
-                latest = jnp.where(ask_in[u // 2, u % 2: u % 2 + 1, :] == lane, u, latest)
-            lastc[0:1, :] = latest
-            lastc_copy.start()
             for n in range(3):
                 two = jnp.broadcast_to(tab[ROW_TWO + n: ROW_TWO + n + 1, :], (vecs, 128)) > 0
                 sums = [
@@ -263,13 +254,20 @@
                 ]
                 t_out[n, 0] = sums[0].astype(BF16)
                 t_out[n, 1] = jnp.where(two, sums[1], 0.0).astype(BF16)
-            ask_copy.wait()
+            for n in range(3):
+                t_sends[n].start()
+            for n in range(3):
+                asks[n].wait()
             for n in range(3):
                 for t in range(2):
-                    x_out[n, t] = xt[ask_s[n, t, 0]]
+                    x_out[n, t] = xt[ask_in[n, t, 0]]
                 x_backs[n].start()
-            for n in range(3):
-                t_sends[n].start()
+            ask_copy.start()
+            latest = jnp.full((1, 128), 6, I32)
+            for u in range(6):
+                latest = jnp.where(ask_in[u // 2, u % 2: u % 2 + 1, :] == lane, u, latest)
+            lastc[0:1, :] = latest
+            lastc_copy.start()
             pl.semaphore_wait(all_x, 3)
             for to in lines[1]:
                 pl.semaphore_signal(all_z, inc=1, device_id=(to, core), device_id_type=MESH)
@@ -323,10 +321,9 @@
         return total + res * res
 
     acc[0:vecs] = lax.fori_loop(0, rows, right_res, jnp.zeros((vecs, 128), F32), unroll=8)
-    right_out = pltpu.make_async_copy(kept, right_hbm, out_sem.at[0])
-    right_out.start()
 
     lastc_copy.wait()
+    ask_copy.wait()
     back[6] = jnp.zeros((vecs, 128), F32)
     for n in range(3):
         t_sends[n].wait()
@@ -344,8 +341,6 @@
         return total + res * res
 
     acc[vecs: 2 * vecs] = lax.fori_loop(0, rows, left_res, jnp.zeros((vecs, 128), F32), unroll=8)
-    left_out = pltpu.make_async_copy(kept_l, left_hbm, out_sem.at[1])
-    left_out.start()
 
     mine = jnp.sum(jnp.transpose(acc[...]), axis=0, keepdims=True)
     mine = jnp.concatenate([mine, jnp.zeros((1, 128 - 2 * vecs), F32)], axis=1)
@@ -365,11 +360,32 @@
         send_sem=n_ss.at[0], recv_sem=n_rs.at[0],
         device_id=(near[0], core), device_id_type=MESH,
     )
+
+    def store(r, _):
+        pltpu.make_async_copy(kept.at[r], right_hbm.at[:, r, 0], out_sem.at[0]).start()
+        pltpu.make_async_copy(kept_l.at[r], left_hbm.at[:, r, 0], out_sem.at[1]).start()
+        return 0
+
+    lax.fori_loop(0, rows, store, 0, unroll=4)
     every.wait_recv()
     every.wait_send()
     norm_ref[...] = jnp.sqrt(jnp.sum(parts[...], axis=0))
-    right_out.wait()
-    left_out.wait()
+    pltpu.make_async_copy(kept, kept, out_sem.at[0]).wait()
+    pltpu.make_async_copy(kept_l, kept_l, out_sem.at[1]).wait()
+
+
+def finish(right, left, norms, right_out, left_out, right_norms, left_norms, sem):
+    copies = [
+        pltpu.make_async_copy(right, right_out, sem.at[0]),
+        pltpu.make_async_copy(left, left_out, sem.at[1]),
+    ]
+    for copy in copies:
+        copy.start()
+    half = right_norms.shape[0]
+    right_norms[...] = norms[0, :half]
+    left_norms[...] = norms[0, half: 2 * half]
+    for copy in copies:
+        copy.wait()
 
 
 def shards(blocks, col_index, right_vecs, left_vecs, ritz):
@@ -382,8 +398,8 @@
     right, left, norms = pl.pallas_call(
         functools.partial(kernel, peers, rows, vecs),
         out_shape=(
-            jax.ShapeDtypeStruct((rows, vecs, width), F32),
-            jax.ShapeDtypeStruct((rows, vecs, width), F32),
+            jax.ShapeDtypeStruct((vecs, rows, 1, width), F32),
+            jax.ShapeDtypeStruct((vecs, rows, 1, width), F32),
             jax.ShapeDtypeStruct((1, 128), F32),
         ),
         in_specs=[any_spec] * 5,
@@ -444,13 +460,20 @@
             )
         )
     )
-    norms = norms[0, : 2 * vecs]
-    return (
-        jnp.swapaxes(right, 0, 1),
-        jnp.swapaxes(left, 0, 1),
-        norms[:vecs],
-        norms[vecs:],
-    )
+    vmem = pl.BlockSpec(memory_space=pltpu.VMEM)
+    return pl.pallas_call(
+        finish,
+        out_shape=(
+            jax.ShapeDtypeStruct((vecs, rows, width), F32),
+            jax.ShapeDtypeStruct((vecs, rows, width), F32),
+            jax.ShapeDtypeStruct((vecs,), F32),
+            jax.ShapeDtypeStruct((vecs,), F32),
+        ),
+        in_specs=[vmem] * 3,
+        out_specs=(any_spec, any_spec, vmem, vmem),
+        scratch_shapes=[dma((2,))],
+        compiler_params=pltpu.CompilerParams(vmem_limit_bytes=8 << 20),
+    )(right.reshape(vecs, rows, width), left.reshape(vecs, rows, width), norms)
 
 
 def solution(mesh):

time: 31.3 us -> 27.9 us (0.89)
  local copies, waits for them, and re-layouts: 3.74 us -> 0 us
    unnamed x2 -> x0, local copies, waits for them, and re-layouts: 3.16 us -> none
    pallas_call x0 -> x1, Pallas kernels: none -> 1.85 us  [shards(): pl.pallas_call(finish, out_shape=(jax.ShapeDtypeStruct((vecs, rows, width...]
    pallas_call x1, Pallas kernels: 26.8 us -> 25.3 us  [shards(): pl.pallas_call(functools.partial(kernel, peers, rows, vecs), out_shape=(j...]
    slice x1 -> x0, local copies, waits for them, and re-layouts: 0.58 us -> none  [shards(): norms[vecs:]]
where the time goes in v4:
time: 27.9 us; the launch traced here: 27.8 us
  Pallas kernels  27.1 us (97%)
  between operations  0.64 us (2%)
    pallas_call x1, Pallas kernels, shards(): pl.pallas_call(functools.partial(kernel, peers, rows, vecs), out_shape=(j...  25.3 us
    pallas_call x1, Pallas kernels, shards(): pl.pallas_call(finish, out_shape=(jax.ShapeDtypeStruct((vecs, rows, width...  1.85 us

profile of v4, /device:TPU:0, one launch (start us, length us, event | category | flops | bytes accessed | tf_op | source)
XLA Modules:
  0.0 27.8 jit_solution(9532803443382575498)
XLA Ops:
  0.6 25.3 %shard_map.84 = (f32[32,64,1,128]{3,2,1,0:T(1,128)S(1)}, f32[32,64,1,128]{3,2,1,0:T(1,128)S(1)}, f32[1,128]{1,0:T(1,128)S(1)}) custom-call(s32[7,64]{1,0:T(8,128)} %bitcast.7, bf16[448,128,128]{2,1,0:T(8,128)(2,1)} %bitcast.6, bf16[32,64,128]{2,1,0:T(8,128)(2,1)} %x_hbm.1, bf16[32,64,128]{2,1,0:T(8,128)(2,1)} %y_hbm.1, bf16[64,64]{1,0:T(8,128)(2,1)} %ritz_hbm.1), custom_call_target="tpu_custom_call" | custom-call | tf_op jit(solution)/shard_map/pallas_call | solution.py:398
  25.9 1.8 %shard_map.85 = (f32[32,64,128]{2,1,0:T(8,128)}, f32[32,64,128]{2,1,0:T(8,128)}, f32[32]{0:T(128)}, f32[32]{0:T(128)}) custom-call(f32[32,64,128]{2,1,0:T(8,128)S(1)} %bitcast.4, f32[32,64,128]{2,1,0:T(8,128)S(1)} %bitcast.5, f32[1,128]{1,0:T(1,128)S(1)} %get-tuple-element.9.norms), custom_call_target="tpu_custom_call" | custom-call | tf_op jit(solution)/shard_map/pallas_call | solution.py:464

commit v5 on v4

--- a/solution.py
+++ b/solution.py
@@ -13,7 +13,7 @@
 I32 = jnp.int32
 SLOTS = 7
 CHUNKS = 8
-PASSES = 4
+SERVE = 5
 OFFSETS = sorted(
     ((a, b, c) for a in range(4) for b in range(4) for c in range(4) if a + b + c),
     key=lambda d: -sum(min(v, 4 - v) for v in d),
@@ -25,11 +25,11 @@
 def kernel(
     peers, rows, vecs,
     cols_hbm, blocks_hbm, x_hbm, y_hbm, ritz_hbm,
-    right_hbm, left_hbm, norm_ref,
+    right, left, norm_ref,
     cols, blk, raw, wide, xt, yt, xo, yo, summed, ritz, shift_r, shift_l,
     tab, tab_s, ask_out, ask_in, ask_s, x_out, x_in, t_out, t_in, back, fixes, lastc, lastc_s,
-    kept, kept_l, acc, parts,
-    in_sem, blk_sem, loc_sem, out_sem,
+    kept, kept_l, turned, parts,
+    in_sem, blk_sem, loc_sem,
     ask_ss, ask_rs, x_ss, x_rs, t_ss, t_rs, o_ss, o_rs, n_ss, n_rs, all_x, all_z,
 ):
     me = lax.axis_index("rows")
@@ -181,15 +181,15 @@
     ins[1].wait()
     by_rows(0, yt)
     y_send = across(yt, yo, 0)
+    ins[2].wait()
+    by_rows(1, xt)
+    x_send = across(xt.at[pl.ds(0, rows)], xo, 1)
     pl.semaphore_wait(barrier, len(met) + 1)
     for copy in asks:
         copy.start()
     for to in lines[0]:
         pl.semaphore_signal(all_x, inc=1, device_id=(to, core), device_id_type=MESH)
     y_send.start()
-    ins[2].wait()
-    by_rows(1, xt)
-    x_send = across(xt.at[pl.ds(0, rows)], xo, 1)
     x_send.start()
 
     ins[3].wait()
@@ -224,7 +224,7 @@
     xt[rows] = jnp.zeros((vecs, 128), BF16)
     tab_copy.wait()
 
-    per_pass = rows // PASSES
+    per_pass = rows // 4
 
     ask_copy = pltpu.make_async_copy(ask_in, ask_s, loc_sem.at[1])
     lastc_copy = pltpu.make_async_copy(lastc, lastc_s, loc_sem.at[2])
@@ -238,11 +238,15 @@
     ]
 
     def one_pass(c, _):
-        for half_pass in range(CHUNKS // PASSES):
-            chunk_copy(c * (CHUNKS // PASSES) + half_pass).wait()
-
-        @pl.when(c == PASSES - 1)
+        @pl.when(c < 3)
         def _():
+            chunk_copy(2 * c).wait()
+            chunk_copy(2 * c + 1).wait()
+
+        @pl.when(c == 3)
+        def _():
+            for last in range(6, CHUNKS):
+                chunk_copy(last).wait()
             for n in range(3):
                 two = jnp.broadcast_to(tab[ROW_TWO + n: ROW_TWO + n + 1, :], (vecs, 128)) > 0
                 sums = [
@@ -291,40 +295,46 @@
         lax.fori_loop(0, per_pass, both, 0, unroll=True)
         return 0
 
-    lax.fori_loop(0, PASSES, one_pass, 0)
+    lax.fori_loop(0, 4, one_pass, 0)
 
     x_send.wait()
     y_send.wait()
 
-    def shifts(r, _):
-        kept[r] += jnp.dot(
+    lastc_copy.wait()
+    ask_copy.wait()
+
+    def shifts(r, totals):
+        res = kept[r] + jnp.dot(
             shift_r[...], jnp.concatenate([xt[r], xo[r]], axis=0), preferred_element_type=F32
         )
-        kept_l[r] = summed[tab_s[ROW_LAST, r]] + jnp.dot(
+        kept[r] = res
+        res_l = summed[tab_s[ROW_LAST, r]] + jnp.dot(
             shift_l[...], jnp.concatenate([yt[r], yo[r]], axis=0), preferred_element_type=F32
         )
-        return 0
-
-    lax.fori_loop(0, rows, shifts, 0, unroll=8)
+        kept_l[r] = res_l
+        return (
+            totals[0] + jnp.where(tab_s[ROW_FIX, r] == 6, res * res, 0.0),
+            totals[1] + jnp.where(lastc_s[0, r] == 6, res_l * res_l, 0.0),
+        )
+
+    zero = jnp.zeros((vecs, 128), F32)
+    right_sq, left_sq = lax.fori_loop(0, rows, shifts, (zero, zero), unroll=16)
+    for u in range(6):
+        turned[u] = blk[tab_s[ROW_PICK + u, 0]].T
 
     for n in range(3):
         x_backs[n].wait()
-    fixes[6] = jnp.zeros((vecs, 128), F32)
+    fixes[6] = zero
     for u in range(6):
-        fixes[u] = lax.dot_general(
-            x_in[u // 2, u % 2], blk[tab_s[ROW_PICK + u, 0]], (((1,), (1,)), ((), ())),
-            preferred_element_type=F32,
-        ) + fixes[tab_s[ROW_SAME + u, 0]]
-    def right_res(r, total):
-        res = kept[r] + fixes[tab_s[ROW_FIX, r]]
-        kept[r] = res
-        return total + res * res
-
-    acc[0:vecs] = lax.fori_loop(0, rows, right_res, jnp.zeros((vecs, 128), F32), unroll=8)
-
-    lastc_copy.wait()
-    ask_copy.wait()
-    back[6] = jnp.zeros((vecs, 128), F32)
+        fix = fixes[tab_s[ROW_SAME + u, 0]] + jnp.dot(
+            x_in[u // 2, u % 2], turned[u], preferred_element_type=F32
+        )
+        fixes[u] = fix
+        at = tab_s[ROW_AT + u, 0]
+        res = kept[at] + fix
+        right_sq += jnp.where(tab_s[ROW_FIX, at] == u, res * res, 0.0)
+
+    back[6] = zero
     for n in range(3):
         t_sends[n].wait()
     for u in range(6):
@@ -334,15 +344,12 @@
                 ask_s[v // 2, v % 2, 0] == ask_s[u // 2, u % 2, 0], jnp.int32(v), prev
             )
         back[u] = t_in[u // 2, u % 2].astype(F32) + back[prev]
-
-    def left_res(c, total):
-        res = kept_l[c] + back[lastc_s[0, c]]
-        kept_l[c] = res
-        return total + res * res
-
-    acc[vecs: 2 * vecs] = lax.fori_loop(0, rows, left_res, jnp.zeros((vecs, 128), F32), unroll=8)
-
-    mine = jnp.sum(jnp.transpose(acc[...]), axis=0, keepdims=True)
+        at = ask_s[u // 2, u % 2, 0]
+        res = kept_l[at] + back[u]
+        left_sq += jnp.where(lastc_s[0, at] == u, res * res, 0.0)
+
+    mine = jnp.concatenate([right_sq, left_sq], axis=0)
+    mine = jnp.sum(jnp.transpose(mine), axis=0, keepdims=True)
     mine = jnp.concatenate([mine, jnp.zeros((1, 128 - 2 * vecs), F32)], axis=1)
     parts[me] = mine
 
@@ -362,28 +369,30 @@
     )
 
     def store(r, _):
-        pltpu.make_async_copy(kept.at[r], right_hbm.at[:, r, 0], out_sem.at[0]).start()
-        pltpu.make_async_copy(kept_l.at[r], left_hbm.at[:, r, 0], out_sem.at[1]).start()
+        right[pl.ds(r, vecs, stride=rows), :] = kept[r] + fixes[tab_s[ROW_FIX, r]]
+        left[pl.ds(r, vecs, stride=rows), :] = kept_l[r] + back[lastc_s[0, r]]
         return 0
 
-    lax.fori_loop(0, rows, store, 0, unroll=4)
+    lax.fori_loop(0, rows, store, 0, unroll=8)
     every.wait_recv()
     every.wait_send()
     norm_ref[...] = jnp.sqrt(jnp.sum(parts[...], axis=0))
-    pltpu.make_async_copy(kept, kept, out_sem.at[0]).wait()
-    pltpu.make_async_copy(kept_l, kept_l, out_sem.at[1]).wait()
-
-
-def finish(right, left, norms, right_out, left_out, right_norms, left_norms, sem):
+
+
+def finish(right, left, norms, right_out, left_out, right_norms, left_norms, first, second, sem):
+    half = right_norms.shape[0]
     copies = [
         pltpu.make_async_copy(right, right_out, sem.at[0]),
         pltpu.make_async_copy(left, left_out, sem.at[1]),
+        pltpu.make_async_copy(first, right_norms, sem.at[2]),
+        pltpu.make_async_copy(second, left_norms, sem.at[3]),
     ]
-    for copy in copies:
-        copy.start()
-    half = right_norms.shape[0]
-    right_norms[...] = norms[0, :half]
-    left_norms[...] = norms[0, half: 2 * half]
+    copies[0].start()
+    copies[1].start()
+    first[...] = norms[0, :half]
+    second[...] = norms[0, half: 2 * half]
+    copies[2].start()
+    copies[3].start()
     for copy in copies:
         copy.wait()
 
@@ -394,16 +403,17 @@
     vecs, _, width = right_vecs.shape
     entries = rows * slots
     any_spec = pl.BlockSpec(memory_space=pl.ANY)
+    vmem = pl.BlockSpec(memory_space=pltpu.VMEM)
     dma = pltpu.SemaphoreType.DMA
     right, left, norms = pl.pallas_call(
         functools.partial(kernel, peers, rows, vecs),
         out_shape=(
-            jax.ShapeDtypeStruct((vecs, rows, 1, width), F32),
-            jax.ShapeDtypeStruct((vecs, rows, 1, width), F32),
+            jax.ShapeDtypeStruct((vecs * rows, width), F32),
+            jax.ShapeDtypeStruct((vecs * rows, width), F32),
             jax.ShapeDtypeStruct((1, 128), F32),
         ),
         in_specs=[any_spec] * 5,
-        out_specs=(any_spec, any_spec, pl.BlockSpec(memory_space=pltpu.VMEM)),
+        out_specs=(vmem,) * 3,
         scratch_shapes=[
             pltpu.VMEM((slots, rows), I32),
             pltpu.VMEM((entries, width, width), BF16),
@@ -432,12 +442,11 @@
             pltpu.SMEM((8, 128), I32),
             pltpu.VMEM((rows, vecs, width), F32),
             pltpu.VMEM((rows, vecs, width), F32),
-            pltpu.VMEM((2 * vecs, width), F32),
+            pltpu.VMEM((6, width, width), BF16),
             pltpu.VMEM((peers, 1, 128), F32),
             dma((4,)),
             dma((CHUNKS,)),
             dma((3,)),
-            dma((2,)),
             dma((3,)), dma((3,)),
             dma((3,)), dma((3,)),
             dma((3,)), dma((3,)),
@@ -460,7 +469,6 @@
             )
         )
     )
-    vmem = pl.BlockSpec(memory_space=pltpu.VMEM)
     return pl.pallas_call(
         finish,
         out_shape=(
@@ -470,8 +478,8 @@
             jax.ShapeDtypeStruct((vecs,), F32),
         ),
         in_specs=[vmem] * 3,
-        out_specs=(any_spec, any_spec, vmem, vmem),
-        scratch_shapes=[dma((2,))],
+        out_specs=(any_spec,) * 4,
+        scratch_shapes=[pltpu.VMEM((vecs,), F32), pltpu.VMEM((vecs,), F32), dma((4,))],
         compiler_params=pltpu.CompilerParams(vmem_limit_bytes=8 << 20),
     )(right.reshape(vecs, rows, width), left.reshape(vecs, rows, width), norms)
 

time: 27.9 us -> 26.2 us (0.939)
  Pallas kernels: 27.1 us -> 25.5 us
    pallas_call x1, Pallas kernels: 25.3 us -> 24.1 us  [shards(): pl.pallas_call(functools.partial(kernel, peers, rows, vecs), out_shape=(j...]
    pallas_call x1, Pallas kernels: 1.85 us -> 1.36 us  [shards(): pl.pallas_call(finish, out_shape=(jax.ShapeDtypeStruct((vecs, rows, width...]
where the time goes in v5:
time: 26.2 us; the launch traced here: 26.1 us
  Pallas kernels  25.5 us (97%)
  between operations  0.64 us (2%)
    pallas_call x1, Pallas kernels, shards(): pl.pallas_call(functools.partial(kernel, peers, rows, vecs), out_shape=(j...  24.1 us
    pallas_call x1, Pallas kernels, shards(): pl.pallas_call(finish, out_shape=(jax.ShapeDtypeStruct((vecs, rows, width...  1.36 us

profile of v5, /device:TPU:0, one launch (start us, length us, event | category | flops | bytes accessed | tf_op | source)
XLA Modules:
  0.0 26.1 jit_solution(13176305386314140745)
XLA Ops:
  0.6 24.1 %shard_map.84 = (f32[2048,128]{1,0:T(8,128)S(1)}, f32[2048,128]{1,0:T(8,128)S(1)}, f32[1,128]{1,0:T(1,128)S(1)}) custom-call(s32[7,64]{1,0:T(8,128)} %bitcast.7, bf16[448,128,128]{2,1,0:T(8,128)(2,1)} %bitcast.6, bf16[32,64,128]{2,1,0:T(8,128)(2,1)} %x_hbm.1, bf16[32,64,128]{2,1,0:T(8,128)(2,1)} %y_hbm.1, bf16[64,64]{1,0:T(8,128)(2,1)} %ritz_hbm.1), custom_call_target="tpu_custom_call" | custom-call | tf_op jit(solution)/shard_map/pallas_call | solution.py:408
  24.8 1.4 %shard_map.85 = (f32[32,64,128]{2,1,0:T(8,128)}, f32[32,64,128]{2,1,0:T(8,128)}, f32[32]{0:T(128)}, f32[32]{0:T(128)}) custom-call(f32[32,64,128]{2,1,0:T(8,128)S(1)} %bitcast.4, f32[32,64,128]{2,1,0:T(8,128)S(1)} %bitcast.5, f32[1,128]{1,0:T(1,128)S(1)} %get-tuple-element.9.norms), custom_call_target="tpu_custom_call" | custom-call | tf_op jit(solution)/shard_map/pallas_call | solution.py:472

commit v6 on v5

--- a/solution.py
+++ b/solution.py
@@ -13,11 +13,7 @@
 I32 = jnp.int32
 SLOTS = 7
 CHUNKS = 8
-SERVE = 5
-OFFSETS = sorted(
-    ((a, b, c) for a in range(4) for b in range(4) for c in range(4) if a + b + c),
-    key=lambda d: -sum(min(v, 4 - v) for v in d),
-)
+ORDER = sorted(range(64), key=lambda p: (p // 16 + p // 4 % 4 + p % 4, p))
 ROW_EXT, ROW_PREV, ROW_LAST, ROW_PICK, ROW_TWO, ROW_SAME, ROW_FIX, ROW_AT = 0, 8, 16, 17, 24, 32, 38, 40
 BACK = (1, 0, 2)
 
@@ -322,18 +318,6 @@
     for u in range(6):
         turned[u] = blk[tab_s[ROW_PICK + u, 0]].T
 
-    for n in range(3):
-        x_backs[n].wait()
-    fixes[6] = zero
-    for u in range(6):
-        fix = fixes[tab_s[ROW_SAME + u, 0]] + jnp.dot(
-            x_in[u // 2, u % 2], turned[u], preferred_element_type=F32
-        )
-        fixes[u] = fix
-        at = tab_s[ROW_AT + u, 0]
-        res = kept[at] + fix
-        right_sq += jnp.where(tab_s[ROW_FIX, at] == u, res * res, 0.0)
-
     back[6] = zero
     for n in range(3):
         t_sends[n].wait()
@@ -348,6 +332,18 @@
         res = kept_l[at] + back[u]
         left_sq += jnp.where(lastc_s[0, at] == u, res * res, 0.0)
 
+    for n in range(3):
+        x_backs[n].wait()
+    fixes[6] = zero
+    for u in range(6):
+        fix = fixes[tab_s[ROW_SAME + u, 0]] + jnp.dot(
+            x_in[u // 2, u % 2], turned[u], preferred_element_type=F32
+        )
+        fixes[u] = fix
+        at = tab_s[ROW_AT + u, 0]
+        res = kept[at] + fix
+        right_sq += jnp.where(tab_s[ROW_FIX, at] == u, res * res, 0.0)
+
     mine = jnp.concatenate([right_sq, left_sq], axis=0)
     mine = jnp.sum(jnp.transpose(mine), axis=0, keepdims=True)
     mine = jnp.concatenate([mine, jnp.zeros((1, 128 - 2 * vecs), F32)], axis=1)
@@ -360,8 +356,8 @@
         )
 
     pl.semaphore_wait(all_z, 3)
-    for offset in OFFSETS:
-        share(peer(offset)).start()
+    for to in ORDER[:-1]:
+        share(jnp.where(me == to, ORDER[-1], to)).start()
     every = pltpu.make_async_remote_copy(
         src_ref=parts.at[pl.ds(0, peers - 1)], dst_ref=parts.at[pl.ds(0, peers - 1)],
         send_sem=n_ss.at[0], recv_sem=n_rs.at[0],

time: 26.2 us -> 26.1 us (level)
  no operation moved by 1% of the time
where the time goes in v6:
time: 26.1 us; the launch traced here: 26 us
  Pallas kernels  25.3 us (97%)
  between operations  0.64 us (2%)
    pallas_call x1, Pallas kernels, shards(): pl.pallas_call(functools.partial(kernel, peers, rows, vecs), out_shape=(j...  24 us
    pallas_call x1, Pallas kernels, shards(): pl.pallas_call(finish, out_shape=(jax.ShapeDtypeStruct((vecs, rows, width...  1.36 us

profile of v6, /device:TPU:0, one launch (start us, length us, event | category | flops | bytes accessed | tf_op | source)
XLA Modules:
  0.0 26.0 jit_solution(15290943738130145298)
XLA Ops:
  0.6 24.0 %shard_map.84 = (f32[2048,128]{1,0:T(8,128)S(1)}, f32[2048,128]{1,0:T(8,128)S(1)}, f32[1,128]{1,0:T(1,128)S(1)}) custom-call(s32[7,64]{1,0:T(8,128)} %bitcast.7, bf16[448,128,128]{2,1,0:T(8,128)(2,1)} %bitcast.6, bf16[32,64,128]{2,1,0:T(8,128)(2,1)} %x_hbm.1, bf16[32,64,128]{2,1,0:T(8,128)(2,1)} %y_hbm.1, bf16[64,64]{1,0:T(8,128)(2,1)} %ritz_hbm.1), custom_call_target="tpu_custom_call" | custom-call | tf_op jit(solution)/shard_map/pallas_call | solution.py:404
  24.6 1.4 %shard_map.85 = (f32[32,64,128]{2,1,0:T(8,128)}, f32[32,64,128]{2,1,0:T(8,128)}, f32[32]{0:T(128)}, f32[32]{0:T(128)}) custom-call(f32[32,64,128]{2,1,0:T(8,128)S(1)} %bitcast.4, f32[32,64,128]{2,1,0:T(8,128)S(1)} %bitcast.5, f32[1,128]{1,0:T(1,128)S(1)} %get-tuple-element.9.norms), custom_call_target="tpu_custom_call" | custom-call | tf_op jit(solution)/shard_map/pallas_call | solution.py:468

commit v7 on v6

--- a/solution.py
+++ b/solution.py
@@ -234,14 +234,14 @@
     ]
 
     def one_pass(c, _):
-        @pl.when(c < 3)
+        @pl.when(c < 2)
         def _():
             chunk_copy(2 * c).wait()
             chunk_copy(2 * c + 1).wait()
 
-        @pl.when(c == 3)
+        @pl.when(c == 2)
         def _():
-            for last in range(6, CHUNKS):
+            for last in range(4, CHUNKS):
                 chunk_copy(last).wait()
             for n in range(3):
                 two = jnp.broadcast_to(tab[ROW_TWO + n: ROW_TWO + n + 1, :], (vecs, 128)) > 0
@@ -256,9 +256,10 @@
                 t_out[n, 1] = jnp.where(two, sums[1], 0.0).astype(BF16)
             for n in range(3):
                 t_sends[n].start()
-            for n in range(3):
-                asks[n].wait()
-            for n in range(3):
+        @pl.when(c == 3)
+        def _():
+            for n in (2, 0, 1):
+                asks[BACK[n]].wait()
                 for t in range(2):
                     x_out[n, t] = xt[ask_in[n, t, 0]]
                 x_backs[n].start()

time: 26.1 us -> 25.9 us (level)
  no operation moved by 1% of the time
where the time goes in v7:
time: 25.9 us; the launch traced here: 25.8 us
  Pallas kernels  25.2 us (97%)
  between operations  0.64 us (2%)
    pallas_call x1, Pallas kernels, shards(): pl.pallas_call(functools.partial(kernel, peers, rows, vecs), out_shape=(j...  23.8 us
    pallas_call x1, Pallas kernels, shards(): pl.pallas_call(finish, out_shape=(jax.ShapeDtypeStruct((vecs, rows, width...  1.36 us

profile of v7, /device:TPU:0, one launch (start us, length us, event | category | flops | bytes accessed | tf_op | source)
XLA Modules:
  0.0 25.8 jit_solution(17681850885322770368)
XLA Ops:
  0.6 23.8 %shard_map.84 = (f32[2048,128]{1,0:T(8,128)S(1)}, f32[2048,128]{1,0:T(8,128)S(1)}, f32[1,128]{1,0:T(1,128)S(1)}) custom-call(s32[7,64]{1,0:T(8,128)} %bitcast.7, bf16[448,128,128]{2,1,0:T(8,128)(2,1)} %bitcast.6, bf16[32,64,128]{2,1,0:T(8,128)(2,1)} %x_hbm.1, bf16[32,64,128]{2,1,0:T(8,128)(2,1)} %y_hbm.1, bf16[64,64]{1,0:T(8,128)(2,1)} %ritz_hbm.1), custom_call_target="tpu_custom_call" | custom-call | tf_op jit(solution)/shard_map/pallas_call | solution.py:405
  24.5 1.4 %shard_map.85 = (f32[32,64,128]{2,1,0:T(8,128)}, f32[32,64,128]{2,1,0:T(8,128)}, f32[32]{0:T(128)}, f32[32]{0:T(128)}) custom-call(f32[32,64,128]{2,1,0:T(8,128)S(1)} %bitcast.4, f32[32,64,128]{2,1,0:T(8,128)S(1)} %bitcast.5, f32[1,128]{1,0:T(1,128)S(1)} %get-tuple-element.9.norms), custom_call_target="tpu_custom_call" | custom-call | tf_op jit(solution)/shard_map/pallas_call | solution.py:469

commit v8 on v6

--- a/solution.py
+++ b/solution.py
@@ -73,7 +73,7 @@
         chunk_copy(c).start()
         return 0
 
-    lax.fori_loop(0, CHUNKS, start_chunk, 0)
+    lax.fori_loop(0, CHUNKS // 2, start_chunk, 0)
 
     ins[0].wait()
     col = cols[...]
@@ -238,6 +238,11 @@
         def _():
             chunk_copy(2 * c).wait()
             chunk_copy(2 * c + 1).wait()
+
+        @pl.when(c < 2)
+        def _():
+            chunk_copy(2 * c + 4).start()
+            chunk_copy(2 * c + 5).start()
 
         @pl.when(c == 3)
         def _():

time: 26.1 us -> 26.1 us (level)
  no operation moved by 1% of the time
where the time goes in v8:
time: 26.1 us; the launch traced here: 26 us
  Pallas kernels  25.3 us (97%)
  between operations  0.64 us (2%)
    pallas_call x1, Pallas kernels, shards(): pl.pallas_call(functools.partial(kernel, peers, rows, vecs), out_shape=(j...  24 us
    pallas_call x1, Pallas kernels, shards(): pl.pallas_call(finish, out_shape=(jax.ShapeDtypeStruct((vecs, rows, width...  1.36 us

profile of v8, /device:TPU:0, one launch (start us, length us, event | category | flops | bytes accessed | tf_op | source)
XLA Modules:
  0.0 26.0 jit_solution(13654954223818300918)
XLA Ops:
  0.6 24.0 %shard_map.84 = (f32[2048,128]{1,0:T(8,128)S(1)}, f32[2048,128]{1,0:T(8,128)S(1)}, f32[1,128]{1,0:T(1,128)S(1)}) custom-call(s32[7,64]{1,0:T(8,128)} %bitcast.7, bf16[448,128,128]{2,1,0:T(8,128)(2,1)} %bitcast.6, bf16[32,64,128]{2,1,0:T(8,128)(2,1)} %x_hbm.1, bf16[32,64,128]{2,1,0:T(8,128)(2,1)} %y_hbm.1, bf16[64,64]{1,0:T(8,128)(2,1)} %ritz_hbm.1), custom_call_target="tpu_custom_call" | custom-call | tf_op jit(solution)/shard_map/pallas_call | solution.py:409
  24.6 1.4 %shard_map.85 = (f32[32,64,128]{2,1,0:T(8,128)}, f32[32,64,128]{2,1,0:T(8,128)}, f32[32]{0:T(128)}, f32[32]{0:T(128)}) custom-call(f32[32,64,128]{2,1,0:T(8,128)S(1)} %bitcast.4, f32[32,64,128]{2,1,0:T(8,128)S(1)} %bitcast.5, f32[1,128]{1,0:T(1,128)S(1)} %get-tuple-element.9.norms), custom_call_target="tpu_custom_call" | custom-call | tf_op jit(solution)/shard_map/pallas_call | solution.py:473
